TPU v7x, 32 devices: a whole 2x2x4 slice. The times are simulated.
32 devices in a mesh: rows: 16 (over z, x, core), cols: 2 (over y).
Axes of the slice: x: 2, y: 2, z: 4, core: 2. Of those that a mesh axis runs over, the one named last changes fastest.
Arguments:
- columns: float32 [16384, 1152], P('rows', 'cols'), may hold values from -4 to 4
- row_bases: float32 [4, 16384, 128], P(None, 'rows'), may hold values from -6 to 6
- order: int32 [16, 1024], P('rows'), may hold values from 0 to 1023, each once within a row
Outputs:
- solved: float32 [16384, 640], P('rows', 'cols')
Inputs may be any that keep to these rules, and one draw needn't show every extreme that they name: Each row of order is a permutation of 0 to 1023.
All inputs are finite; a program needn't handle non-finite values.
Results may differ from a plain program's by a relative error of at most 0.01.
Values sent between devices are 32-bit elements; how exact they have to be, the bound alone decides.
A program may use at most 64 MiB of HBM per device.

v0:
```python
import math

import jax
import jax.numpy as jnp
from jax import lax
from jax.sharding import PartitionSpec as P

R = 128
LEVELS = 4
TGT_DEV = 320


HIGH = lax.Precision.HIGHEST


def partner(block, axis, apart):
    count = lax.axis_size(axis)
    route = []
    for low in range(count):
        high = low | 1 << apart
        if high != low and high < count:
            route += [(low, high), (high, low)]
    return lax.ppermute(block, axis, route)


def solve_system(coupled, right_side):
    gram = jnp.einsum("ki,kj->ij", coupled, coupled, precision=HIGH)
    factor = jnp.linalg.cholesky(gram)
    projected = jnp.einsum("ki,kq->iq", coupled, right_side, precision=HIGH)
    middle = lax.linalg.triangular_solve(factor, projected, left_side=True, lower=True)
    return lax.linalg.triangular_solve(factor, middle, left_side=True, lower=True, transpose_a=True)


def whole_sums(partial_value, bits):
    for step in range(bits):
        partial_value = partial_value + partner(partial_value, "rows", step)
    return (partial_value, partner(partial_value, "rows", bits))


def on_device(columns, row_bases, order):
    rows_dev = columns.shape[0]
    row_count = lax.axis_size("rows")
    col_count = lax.axis_size("cols")
    width_block = R // col_count
    depth = row_count.bit_length() - 1
    position = lax.axis_index("rows")
    places = order[0]
    tree = jnp.take(columns, places, axis=0)
    for level in range(LEVELS):
        bits = depth - LEVELS + level
        scale = 0.55 / math.sqrt(R * rows_dev * (1 << bits))
        start = TGT_DEV + (LEVELS - 1 - level) * width_block
        upper = tree[:, :start]
        basis = lax.all_gather(tree[:, start : start + width_block], "cols", axis=1, tiled=True)
        feats = row_bases[level]
        partial_value = scale * jnp.einsum(
            "cr,cq->rq", feats, tree[:, : start + width_block], precision=HIGH
        )
        own_sum, sibling = whole_sums(partial_value, bits)
        own_proj, sibling_proj = (own_sum[:, :start], sibling[:, :start])
        own_couple, sibling_couple = (own_sum[:, start:], sibling[:, start:])
        own_couple, sibling_couple = (
            lax.all_gather(own_couple, "cols", axis=1, tiled=True),
            lax.all_gather(sibling_couple, "cols", axis=1, tiled=True),
        )
        first_child = position >> bits & 1 == 0
        couple_a = jnp.where(first_child, own_couple, sibling_couple)
        couple_b = jnp.where(first_child, sibling_couple, own_couple)
        proj_a = jnp.where(first_child, own_proj, sibling_proj)
        proj_b = jnp.where(first_child, sibling_proj, own_proj)
        ident = jnp.eye(R, dtype=couple_a.dtype)
        system = jnp.concatenate(
            [
                jnp.concatenate([ident, couple_b], axis=1),
                jnp.concatenate([couple_a, ident], axis=1),
            ],
            axis=0,
        )
        coeffs = solve_system(system, jnp.concatenate([proj_b, proj_a], axis=0))
        mine = jnp.where(first_child, coeffs[:R], coeffs[R:])
        upper = upper - jnp.dot(basis, mine, precision=HIGH)
        tree = jnp.concatenate([upper, tree[:, start:]], axis=1)
    targets = tree[:, :TGT_DEV]
    return jnp.zeros_like(targets).at[places].set(targets)


def solution(mesh):
    placed = (P("rows", "cols"), P(None, "rows", None), P("rows", None))
    return jax.shard_map(
        on_device, mesh=mesh, in_specs=placed, out_specs=P("rows", "cols"), check_vma=False
    )
```

profile of v0, /device:TPU:0, one launch (start us, length us, event | category | flops | bytes accessed | tf_op | source)
XLA Modules:
  0.0 413.2 jit_solution(978485674715945355)
XLA Ops:
  0.7 2.1 copy.12
  2.8 5.2 %gather_fusion = f32[1024,576]{1,0:T(8,128)} fusion(f32[1024,576]{1,0:T(8,128)S(1)} %copy.12, s32[1024]{0:T(1024)S(1)} %broadcast_clamp_fusion), kind=kCustom, calls=%fused_computation | custom fusion | bytes 4722688 | tf_op jit(solution)/shard_map/jit(_take)/gather | solution.py:48
  8.0 3.2 copy.13
  11.2 1.9 broadcast_select_fusion
  13.1 3.8 fusion
  18.1 5.2 %all_gather.38 = f32[128,128]{0,1:T(8,128)S(1)} all-gather(f32[128,64]{0,1:T(8,128)S(1)} %slice.272), channel_id=1, replica_groups=mesh['rows'=16,'cols'=2] {'cols'}, dimensions={1}, use_global_device_ids=true | all-gather | bytes 98304 | tf_op jit(solution)/shard_map/all_gather | solution.py:63
  23.3 8.8 %all_gather.36 = f32[1024,128]{0,1:T(8,128)S(1)} all-gather(f32[1024,64]{0,1:T(8,128)S(1)} %slice.270), channel_id=1, replica_groups=mesh['rows'=16,'cols'=2] {'cols'}, dimensions={1}, use_global_device_ids=true | all-gather | bytes 786432 | tf_op jit(solution)/shard_map/all_gather | solution.py:54
  32.9 4.9 %all_gather.37 = f32[128,128]{0,1:T(8,128)S(1)} all-gather(f32[128,64]{0,1:T(8,128)S(1)} %slice.271), channel_id=1, replica_groups=mesh['rows'=16,'cols'=2] {'cols'}, dimensions={1}, use_global_device_ids=true | all-gather | bytes 98304 | tf_op jit(solution)/shard_map/all_gather | solution.py:64
  39.7 11.7 %cholesky.214 = f32[128,128]{1,0:T(8,128)S(1)} custom-call(f32[128,128]{1,0:T(8,128)S(1)} %cholesky.346), custom_call_target="Cholesky" | custom-call | tf_op jit(solution)/shard_map/jit(cholesky)/cholesky | solution.py:28
  51.4 9.8 %custom-call.35 = f32[1,128,128]{1,2,0:T(8,128)S(1)} custom-call(f32[1,128,128]{2,1,0:T(8,128)S(1)} %get-tuple-element.109), custom_call_target="InvertDiagBlocksLowerTriangular" | custom-call | tf_op jit(solution)/shard_map/jit(cholesky)/cholesky | solution.py:28
  63.4 11.7 %cholesky.231 = f32[128,128]{1,0:T(8,128)S(1)} custom-call(f32[128,128]{1,0:T(8,128)S(1)} %convolution_subtract_fusion.12), custom_call_target="Cholesky" | custom-call | tf_op jit(solution)/shard_map/jit(cholesky)/cholesky | solution.py:28
  77.3 4.4 %while.4 = (s32[]{:T(128)}, f32[256,256]{1,0:T(8,128)S(1)}, s32[2,2]{1,0:T(2,128)S(1)}, f32[2,128,128]{2,1,0:T(8,128)S(1)}, s32[]{:T(128)}) while((s32[]{:T(128)}, f32[256,256]{1,0:T(8,128)S(1)}, s32[2,2]{1,0:T(2,128)S(1)}, f32[2,128,128]{2,1,0:T(8,128)S(1)}, s32[]{:T(128)}) %tuple.83), condition=%wide.while_cond, body=%wide.while_body.sunk | while | flops 2 | bytes 131181 | solution.py:31
  81.7 20.3 %custom-call.28 = f32[2,128,128]{1,2,0:T(8,128)} custom-call(f32[2,128,128]{2,1,0:T(8,128)S(1)} %get-tuple-element.13), custom_call_target="InvertDiagBlocksLowerTriangular" | custom-call | tf_op jit(solution)/shard_map/triangular_solve | solution.py:31
  109.0 1.8 slice_subtract_fusion
  112.2 2.8 fusion.1
  119.0 8.7 %all_gather.39 = f32[1024,128]{0,1:T(8,128)S(1)} all-gather(f32[1024,64]{0,1:T(8,128)S(1)} %slice.276), channel_id=1, replica_groups=mesh['rows'=16,'cols'=2] {'cols'}, dimensions={1}, use_global_device_ids=true | all-gather | bytes 786432 | tf_op jit(solution)/shard_map/all_gather | solution.py:54
  127.7 4.6 %all_gather.41 = f32[128,128]{0,1:T(8,128)S(1)} all-gather(f32[128,64]{0,1:T(8,128)S(1)} %slice.278), channel_id=1, replica_groups=mesh['rows'=16,'cols'=2] {'cols'}, dimensions={1}, use_global_device_ids=true | all-gather | bytes 98304 | tf_op jit(solution)/shard_map/all_gather | solution.py:63
  132.3 4.8 %all_gather.40 = f32[128,128]{0,1:T(8,128)S(1)} all-gather(f32[128,64]{0,1:T(8,128)S(1)} %slice.277), channel_id=1, replica_groups=mesh['rows'=16,'cols'=2] {'cols'}, dimensions={1}, use_global_device_ids=true | all-gather | bytes 98304 | tf_op jit(solution)/shard_map/all_gather | solution.py:64
  137.7 11.7 %cholesky.248 = f32[128,128]{1,0:T(8,128)S(1)} custom-call(f32[128,128]{1,0:T(8,128)S(1)} %cholesky.349), custom_call_target="Cholesky" | custom-call | tf_op jit(solution)/shard_map/jit(cholesky)/cholesky | solution.py:28
  149.5 9.8 %custom-call.36 = f32[1,128,128]{1,2,0:T(8,128)S(1)} custom-call(f32[1,128,128]{2,1,0:T(8,128)S(1)} %get-tuple-element.105), custom_call_target="InvertDiagBlocksLowerTriangular" | custom-call | tf_op jit(solution)/shard_map/jit(cholesky)/cholesky | solution.py:28
  159.8 11.7 %cholesky.265 = f32[128,128]{1,0:T(8,128)S(1)} custom-call(f32[128,128]{1,0:T(8,128)S(1)} %convolution_subtract_fusion.11), custom_call_target="Cholesky" | custom-call | tf_op jit(solution)/shard_map/jit(cholesky)/cholesky | solution.py:28
  174.1 4.1 %while.5 = (s32[]{:T(128)}, f32[256,256]{1,0:T(8,128)S(1)}, s32[2,2]{1,0:T(2,128)S(1)}, f32[2,128,128]{2,1,0:T(8,128)S(1)}, s32[]{:T(128)}) while((s32[]{:T(128)}, f32[256,256]{1,0:T(8,128)S(1)}, s32[2,2]{1,0:T(2,128)S(1)}, f32[2,128,128]{2,1,0:T(8,128)S(1)}, s32[]{:T(128)}) %tuple.95), condition=%wide.while_cond.1, body=%wide.while_body.1.sunk | while | flops 2 | bytes 131181 | solution.py:31
  178.3 19.7 %custom-call.29 = f32[2,128,128]{1,2,0:T(8,128)S(1)} custom-call(f32[2,128,128]{2,1,0:T(8,128)S(1)} %get-tuple-element.21), custom_call_target="InvertDiagBlocksLowerTriangular" | custom-call | tf_op jit(solution)/shard_map/triangular_solve | solution.py:31
  202.7 2.6 fusion.2
  207.7 6.9 %collective-permute-done.4 = f32[128,448]{0,1:T(8,128)S(1)} collective-permute-done((f32[128,448]{0,1:T(8,128)S(1)}, f32[128,448]{0,1:T(8,128)S(1)}, u32[]{:S(2)}, u32[]{:S(2)}) %collective-permute-start.4) | collective-permute-done | bytes 229408 | tf_op jit(solution)/shard_map/ppermute | solution.py:23
  214.6 1.6 collective-permute-start.5
  216.3 8.0 %all_gather.42 = f32[1024,128]{0,1:T(8,128)} all-gather(f32[1024,64]{0,1:T(8,128)S(1)} %slice.282), channel_id=1, replica_groups=mesh['rows'=16,'cols'=2] {'cols'}, dimensions={1}, use_global_device_ids=true | all-gather | bytes 786432 | tf_op jit(solution)/shard_map/all_gather | solution.py:54
  224.3 4.6 %all_gather.44 = f32[128,128]{0,1:T(8,128)S(1)} all-gather(f32[128,64]{0,1:T(8,128)S(1)} %slice.284), channel_id=1, replica_groups=mesh['rows'=16,'cols'=2] {'cols'}, dimensions={1}, use_global_device_ids=true | all-gather | bytes 98304 | tf_op jit(solution)/shard_map/all_gather | solution.py:63
  228.9 5.0 %all_gather.43 = f32[128,128]{0,1:T(8,128)S(1)} all-gather(f32[128,64]{0,1:T(8,128)S(1)} %slice.283), channel_id=1, replica_groups=mesh['rows'=16,'cols'=2] {'cols'}, dimensions={1}, use_global_device_ids=true | all-gather | bytes 98304 | tf_op jit(solution)/shard_map/all_gather | solution.py:64
  234.6 11.7 %cholesky.282 = f32[128,128]{1,0:T(8,128)S(1)} custom-call(f32[128,128]{1,0:T(8,128)S(1)} %cholesky.352), custom_call_target="Cholesky" | custom-call | tf_op jit(solution)/shard_map/jit(cholesky)/cholesky | solution.py:28
  246.3 9.8 %custom-call.37 = f32[1,128,128]{1,2,0:T(8,128)S(1)} custom-call(f32[1,128,128]{2,1,0:T(8,128)S(1)} %get-tuple-element.101), custom_call_target="InvertDiagBlocksLowerTriangular" | custom-call | tf_op jit(solution)/shard_map/jit(cholesky)/cholesky | solution.py:28
  256.6 11.7 %cholesky.299 = f32[128,128]{1,0:T(8,128)S(1)} custom-call(f32[128,128]{1,0:T(8,128)S(1)} %convolution_subtract_fusion.10), custom_call_target="Cholesky" | custom-call | tf_op jit(solution)/shard_map/jit(cholesky)/cholesky | solution.py:28
  271.0 4.0 while.6
  275.0 19.7 %custom-call.30 = f32[2,128,128]{1,2,0:T(8,128)S(1)} custom-call(f32[2,128,128]{2,1,0:T(8,128)S(1)} %get-tuple-element.29), custom_call_target="InvertDiagBlocksLowerTriangular" | custom-call | tf_op jit(solution)/shard_map/triangular_solve | solution.py:31
  298.6 2.4 slice_subtract_fusion.2
  301.1 2.4 fusion.3
  305.6 6.4 %collective-permute-done.7 = f32[128,384]{0,1:T(8,128)S(1)} collective-permute-done((f32[128,384]{0,1:T(8,128)S(1)}, f32[128,384]{0,1:T(8,128)S(1)}, u32[]{:S(2)}, u32[]{:S(2)}) %collective-permute-start.7) | collective-permute-done | bytes 196640 | tf_op jit(solution)/shard_map/ppermute | solution.py:23
  312.6 5.7 %collective-permute-done.8 = f32[128,384]{0,1:T(8,128)S(1)} collective-permute-done((f32[128,384]{0,1:T(8,128)S(1)}, f32[128,384]{0,1:T(8,128)S(1)}, u32[]{:S(2)}, u32[]{:S(2)}) %collective-permute-start.8) | collective-permute-done | bytes 196640 | tf_op jit(solution)/shard_map/ppermute | solution.py:23
  318.3 2.8 collective-permute-start.9
  321.1 7.0 %all_gather.45 = f32[1024,128]{0,1:T(8,128)S(1)} all-gather(f32[1024,64]{0,1:T(8,128)S(1)} %slice.288), channel_id=1, replica_groups=mesh['rows'=16,'cols'=2] {'cols'}, dimensions={1}, use_global_device_ids=true | all-gather | bytes 786432 | tf_op jit(solution)/shard_map/all_gather | solution.py:54
  328.1 4.6 %all_gather.47 = f32[128,128]{0,1:T(8,128)S(1)} all-gather(f32[128,64]{0,1:T(8,128)S(1)} %slice.290), channel_id=1, replica_groups=mesh['rows'=16,'cols'=2] {'cols'}, dimensions={1}, use_global_device_ids=true | all-gather | bytes 98304 | tf_op jit(solution)/shard_map/all_gather | solution.py:63
  333.4 4.8 %all_gather.46 = f32[128,128]{0,1:T(8,128)S(1)} all-gather(f32[128,64]{0,1:T(8,128)S(1)} %slice.289), channel_id=1, replica_groups=mesh['rows'=16,'cols'=2] {'cols'}, dimensions={1}, use_global_device_ids=true | all-gather | bytes 98304 | tf_op jit(solution)/shard_map/all_gather | solution.py:64
  338.8 11.7 %cholesky.316 = f32[128,128]{1,0:T(8,128)S(1)} custom-call(f32[128,128]{1,0:T(8,128)S(1)} %cholesky.355), custom_call_target="Cholesky" | custom-call | tf_op jit(solution)/shard_map/jit(cholesky)/cholesky | solution.py:28
  350.6 9.8 %custom-call.38 = f32[1,128,128]{1,2,0:T(8,128)S(1)} custom-call(f32[1,128,128]{2,1,0:T(8,128)S(1)} %get-tuple-element.97), custom_call_target="InvertDiagBlocksLowerTriangular" | custom-call | tf_op jit(solution)/shard_map/jit(cholesky)/cholesky | solution.py:28
  360.9 11.7 %cholesky.333 = f32[128,128]{1,0:T(8,128)S(1)} custom-call(f32[128,128]{1,0:T(8,128)S(1)} %convolution_subtract_fusion.9), custom_call_target="Cholesky" | custom-call | tf_op jit(solution)/shard_map/jit(cholesky)/cholesky | solution.py:28
  375.3 4.3 %while.7 = (s32[]{:T(128)}, f32[256,256]{1,0:T(8,128)S(1)}, s32[2,2]{1,0:T(2,128)S(1)}, f32[2,128,128]{2,1,0:T(8,128)S(1)}, s32[]{:T(128)}) while((s32[]{:T(128)}, f32[256,256]{1,0:T(8,128)S(1)}, s32[2,2]{1,0:T(2,128)S(1)}, f32[2,128,128]{2,1,0:T(8,128)S(1)}, s32[]{:T(128)}) %tuple.97), condition=%wide.while_cond.3, body=%wide.while_body.3.sunk | while | flops 2 | bytes 131181 | solution.py:31
  379.6 19.7 %custom-call.31 = f32[2,128,128]{1,2,0:T(8,128)S(1)} custom-call(f32[2,128,128]{2,1,0:T(8,128)S(1)} %get-tuple-element.37), custom_call_target="InvertDiagBlocksLowerTriangular" | custom-call | tf_op jit(solution)/shard_map/triangular_solve | solution.py:31
  405.7 5.8 %scatter_custom_fusion = f32[1024,320]{1,0:T(8,128)S(1)} fusion(s32[1024]{0:T(1024)S(1)} %bitcast.182, f32[1024,320]{1,0:T(8,128)} %copy.20, f32[]{:T(128)} %constant.125.clone.1), kind=kCustom, calls=%fused_computation.39 | custom fusion | bytes 1311232 | tf_op jit(solution)/shard_map/scatter | solution.py:84
  (172 shorter events, 65.2 us)
Async XLA Ops:
  8.0 3.2 copy-start.7
  16.8 15.3 %collective-permute-start = (f32[128,576]{0,1:T(8,128)}, f32[128,576]{0,1:T(8,128)}, u32[]{:S(2)}, u32[]{:S(2)}) collective-permute-start(f32[128,576]{0,1:T(8,128)} %fusion), channel_id=1, source_target_pairs={{0,2},{2,0},{4,6},{6,4},{8,10},{10,8},{12,14},{14,12},{16,18},{18,... | collective-permute-start | bytes 884744 | tf_op jit(solution)/shard_map/ppermute | solution.py:23
  37.8 0.6 copy-start.4
  39.0 0.7 copy-start.2
  102.0 2.6 copy-start.3
  110.8 1.4 copy-start
  115.0 1.6 collective-permute-start.1
  116.7 15.6 %collective-permute-start.2 = (f32[128,512]{0,1:T(8,128)S(1)}, f32[128,512]{0,1:T(8,128)S(1)}, u32[]{:S(2)}, u32[]{:S(2)}) collective-permute-start(f32[128,512]{0,1:T(8,128)S(1)} %add.77), channel_id=1, source_target_pairs={{0,4},{4,0},{2,6},{6,2},{8,12},{12,8},{10,14},{14,10},{16,20},{20,... | collective-permute-start | bytes 786440 | tf_op jit(solution)/shard_map/ppermute | solution.py:23
  198.6 2.5 copy-start.1
  205.3 1.6 collective-permute-start.3
  206.9 7.7 %collective-permute-start.4 = (f32[128,448]{0,1:T(8,128)S(1)}, f32[128,448]{0,1:T(8,128)S(1)}, u32[]{:S(2)}, u32[]{:S(2)}) collective-permute-start(f32[128,448]{0,1:T(8,128)S(1)} %add.78), channel_id=1, source_target_pairs={{0,4},{4,0},{2,6},{6,2},{8,12},{12,8},{10,14},{14,10},{16,20},{20,... | collective-permute-start | bytes 688136 | tf_op jit(solution)/shard_map/ppermute | solution.py:23
  214.6 14.3 %collective-permute-start.5 = (f32[128,448]{0,1:T(8,128)S(1)}, f32[128,448]{0,1:T(8,128)S(1)}, u32[]{:S(2)}, u32[]{:S(2)}) collective-permute-start(f32[128,448]{0,1:T(8,128)S(1)} %add.79), channel_id=1, source_target_pairs={{0,8},{8,0},{2,10},{10,2},{4,12},{12,4},{6,14},{14,6},{16,24},{24,... | collective-permute-start | bytes 688136 | tf_op jit(solution)/shard_map/ppermute | solution.py:23
  228.9 5.0 %copy-start.5 = (f32[128,448]{0,1:T(8,128)}, f32[128,448]{0,1:T(8,128)S(1)}, u32[]{:S(2)}) copy-start(f32[128,448]{0,1:T(8,128)S(1)} %collective-permute-done.5) | copy-start | bytes 688132
  303.5 1.5 collective-permute-start.6
  305.0 7.0 %collective-permute-start.7 = (f32[128,384]{0,1:T(8,128)S(1)}, f32[128,384]{0,1:T(8,128)S(1)}, u32[]{:S(2)}, u32[]{:S(2)}) collective-permute-start(f32[128,384]{0,1:T(8,128)S(1)} %add.80), channel_id=1, source_target_pairs={{0,4},{4,0},{2,6},{6,2},{8,12},{12,8},{10,14},{14,10},{16,20},{20,... | collective-permute-start | bytes 589832 | tf_op jit(solution)/shard_map/ppermute | solution.py:23
  312.1 6.2 %collective-permute-start.8 = (f32[128,384]{0,1:T(8,128)S(1)}, f32[128,384]{0,1:T(8,128)S(1)}, u32[]{:S(2)}, u32[]{:S(2)}) collective-permute-start(f32[128,384]{0,1:T(8,128)S(1)} %add.81), channel_id=1, source_target_pairs={{0,8},{8,0},{2,10},{10,2},{4,12},{12,4},{6,14},{14,6},{16,24},{24,... | collective-permute-start | bytes 589832 | tf_op jit(solution)/shard_map/ppermute | solution.py:23
  318.3 14.4 %collective-permute-start.9 = (f32[128,384]{0,1:T(8,128)S(1)}, f32[128,384]{0,1:T(8,128)S(1)}, u32[]{:S(2)}, u32[]{:S(2)}) collective-permute-start(f32[128,384]{0,1:T(8,128)S(1)} %add.82), channel_id=1, source_target_pairs={{0,16},{16,0},{2,18},{18,2},{4,20},{20,4},{6,22},{22,6},{8,24},{24... | collective-permute-start | bytes 589832 | tf_op jit(solution)/shard_map/ppermute | solution.py:23
  332.7 0.7 copy-start.6
where the time goes:
time: 418 us; the launch traced here: 413 us
  other arithmetic  223 us (53%)
  blocking collectives  71 us (17%)
  local copies, waits for them, and re-layouts  41.7 us (10%)
  matrix products  38 us (9%)
  waiting for transfers between devices  23.4 us (6%)
  starting transfers between devices  8.32 us (2%)
  between operations  6.02 us (1%)
    another operation x27, other arithmetic, solve_system(): factor = jnp.linalg.cholesky(gram)  138 us
    another operation x9, other arithmetic, solve_system(): lax.linalg.triangular_solve(factor, middle, left_side=True, lower=True, t...  79.4 us
    all_gather x4, blocking collectives, on_device(): lax.all_gather(tree[:, start:start + width_block], 'cols', axis=1, tiled=...  32.6 us
    ppermute x10, waiting for transfers between devices, partner(): return lax.ppermute(block, axis, route)  23.4 us
    all_gather x4, blocking collectives, on_device(): lax.all_gather(sibling_couple, 'cols', axis=1, tiled=True)  19.4 us
    all_gather x4, blocking collectives, on_device(): lax.all_gather(own_couple, 'cols', axis=1, tiled=True)  19 us
    another operation x24, local copies, waits for them, and re-layouts  15.5 us
    dot_general x4, matrix products, on_device(): jnp.einsum('cr,cq->rq', feats, tree[:, :start + width_block], precision=H...  11.7 us
  transfers between devices with their start and end apart: 10, of which 6 were waited for; matrix products, arithmetic and copies ran while one was open for 0% of the time, Pallas kernels for 0%

commit v1 on v0

v1 whole, which is shorter than its diff:
```python
import functools
import math

import jax
import jax.numpy as jnp
from jax import lax
from jax.experimental import pallas as pl
from jax.experimental.pallas import tpu as pltpu
from jax.sharding import PartitionSpec as P

R = 128
LEVELS = 4
TGT_DEV = 320
LANES = 128
TGT_PAD = -(-TGT_DEV // LANES) * LANES
VMEM_BYTES = 48 * 1024 * 1024
F32 = jnp.float32
BF16 = jnp.bfloat16

ROWS_ON_COLS = (((1,), (0,)), ((), ()))
COLS_ON_COLS = (((0,), (0,)), ((), ()))


def halves(value):
    high = value.astype(BF16)
    return high, (value - high.astype(F32)).astype(BF16)


def mul_halves(left, right, dims=ROWS_ON_COLS):
    def one(a, b):
        return lax.dot_general(a, b, dims, preferred_element_type=F32)

    return one(left[0], right[0]) + (one(left[0], right[1]) + one(left[1], right[0]))


def mul(left, right):
    return mul_halves(halves(left), halves(right))


def mul_full(left, right, dims=ROWS_ON_COLS):
    return lax.dot_general(
        left, right, dims, precision=lax.Precision.HIGHEST, preferred_element_type=F32
    )


def invert_two(a, b, d):
    ia = 1.0 / a
    t = b * ia
    low = 1.0 / (d - b * t)
    mid = -t * low
    return ia - t * mid, mid, low


def invert_four(d):
    e00, e01, e11 = invert_two(d[0][0], d[0][1], d[1][1])
    f00, f01, f10, f11 = d[0][2], d[0][3], d[1][2], d[1][3]
    w00, w01 = e00 * f00 + e01 * f10, e00 * f01 + e01 * f11
    w10, w11 = e01 * f00 + e11 * f10, e01 * f01 + e11 * f11
    s00 = d[2][2] - (f00 * w00 + f10 * w10)
    s01 = d[2][3] - (f00 * w01 + f10 * w11)
    s11 = d[3][3] - (f01 * w01 + f11 * w11)
    g00, g01, g11 = invert_two(s00, s01, s11)
    u00, u01 = w00 * g00 + w01 * g01, w00 * g01 + w01 * g11
    u10, u11 = w10 * g00 + w11 * g01, w10 * g01 + w11 * g11
    t00 = e00 + u00 * w00 + u01 * w01
    t01 = e01 + u00 * w10 + u01 * w11
    t11 = e11 + u10 * w10 + u11 * w11
    return [
        [t00, t01, -u00, -u01],
        [t01, t11, -u10, -u11],
        [-u00, -u10, g00, g01],
        [-u01, -u11, g01, g11],
    ]


def sweep_four(tiles, first):
    lane = lax.broadcasted_iota(jnp.int32, (8, LANES), 1)
    sub = lax.broadcasted_iota(jnp.int32, (8, LANES), 0)
    spread = [
        [jnp.broadcast_to(tile[:, first + j : first + j + 1], (8, LANES)) for j in range(4)]
        for tile in tiles
    ]
    pivot = [
        [jnp.broadcast_to(spread[0][j][first + i : first + i + 1], (8, LANES)) for j in range(4)]
        for i in range(4)
    ]
    inverse = invert_four(pivot)
    rows = [
        jnp.where(
            (lane >= first) & (lane < first + 4),
            jnp.where(lane == first + j, 1.0, 0.0),
            jnp.broadcast_to(tiles[0][first + j : first + j + 1], (8, LANES)),
        )
        for j in range(4)
    ]
    solved = [
        (inverse[i][0] * rows[0] + inverse[i][1] * rows[1])
        + (inverse[i][2] * rows[2] + inverse[i][3] * rows[3])
        for i in range(4)
    ]
    kept = (lane < first) | (lane >= first + 4)
    out = []
    for tile, cols in zip(tiles, spread):
        change = (cols[0] * solved[0] + cols[1] * solved[1]) + (
            cols[2] * solved[2] + cols[3] * solved[3]
        )
        out.append(jnp.where(kept, tile, 0.0) - change)
    for i in range(4):
        out[0] = jnp.where(sub == first + i, solved[i], out[0])
    return out


def invert_spd(gram):
    count = R // 8

    def body(_, tiles):
        tiles = sweep_four(list(tiles), 0)
        tiles = sweep_four(tiles, 4)
        tiles = tiles[1:] + tiles[:1]
        return tuple(pltpu.roll(tile, LANES - 8, 1) for tile in tiles)

    tiles = tuple(gram[8 * i : 8 * i + 8] for i in range(count))
    return jnp.concatenate(lax.fori_loop(0, count, body, tiles), axis=0)


def solve_own(own_couple, sib_couple, own_proj, sib_proj):
    row = lax.broadcasted_iota(jnp.int32, (R, R), 0)
    col = lax.broadcasted_iota(jnp.int32, (R, R), 1)
    reduced = jnp.where(row == col, 1.0, 0.0) - mul_full(sib_couple, own_couple)
    inverse = invert_spd(mul_full(reduced, reduced, COLS_ON_COLS))
    right = sib_proj - mul(sib_couple, own_proj)
    return mul_full(mul_full(inverse, reduced, (((1,), (1,)), ((), ()))), right)


def project_kernel(scales, cols_ref, basis_ref, bases_ref, order_ref, tgt_ref, own_ref):
    rows = cols_ref.shape[0]
    place = lax.broadcasted_iota(jnp.int32, (rows, rows), 0)
    pick = jnp.where(place == order_ref[...], 1.0, 0.0).astype(BF16)
    tgt = halves(cols_ref[:, :TGT_PAD])
    basis = halves(basis_ref[...])
    for level in range(LEVELS):
        high, low = halves(bases_ref[level])
        high = jnp.dot(pick, high, preferred_element_type=F32).astype(BF16)
        low = jnp.dot(pick, low, preferred_element_type=F32).astype(BF16)
        at = pl.ds(level * R, R)
        tgt_ref[at, :] = scales[level] * mul_halves((high, low), tgt, COLS_ON_COLS)
        own_ref[at, :] = scales[level] * mul_halves((high, low), basis, COLS_ON_COLS)


def project(scales, columns, basis, row_bases, order):
    return pl.pallas_call(
        functools.partial(project_kernel, scales),
        out_shape=(
            jax.ShapeDtypeStruct((LEVELS * R, TGT_PAD), F32),
            jax.ShapeDtypeStruct((LEVELS * R, basis.shape[1]), F32),
        ),
        compiler_params=pltpu.CompilerParams(vmem_limit_bytes=VMEM_BYTES),
    )(columns, basis, row_bases, order)


def spread_level(block, level, width, source):
    offset = (LEVELS - 1 - level) * width
    tile = block[:, offset // LANES * LANES : offset // LANES * LANES + LANES]
    shift = lax.rem(source * width - offset % LANES + LANES, LANES)
    lane = lax.broadcasted_iota(jnp.int32, tile.shape, 1)
    inside = (lane >= source * width) & (lane < (source + 1) * width)
    return jnp.where(inside, pltpu.roll(tile, shift, 1), 0.0)


def assemble_kernel(count, *refs):
    out_ref, width = refs[-1], R // count
    me = lax.axis_index("cols")
    for level in range(LEVELS):
        total = None
        for apart in range(count):
            part = spread_level(refs[apart][...], level, width, lax.rem(me - apart + count, count))
            total = part if total is None else total + part
        out_ref[:, level * R : (level + 1) * R] = total


def assemble(count, blocks):
    return pl.pallas_call(
        functools.partial(assemble_kernel, count),
        out_shape=jax.ShapeDtypeStruct((LEVELS * R, LEVELS * R), F32),
        compiler_params=pltpu.CompilerParams(vmem_limit_bytes=VMEM_BYTES),
    )(*blocks)


def level_kernel(own_ref, sib_ref, rest_ref, coeff_ref, out_ref):
    coeffs = solve_own(own_ref[:, :R], sib_ref[:, :R], own_ref[:, R:], sib_ref[:, R:])
    coeff_ref[...] = coeffs
    out_ref[...] = rest_ref[:, R:] - mul(rest_ref[:, :R], coeffs)


def last_kernel(own_ref, sib_ref, coeff_ref):
    coeff_ref[...] = solve_own(own_ref[:, :R], sib_ref[:, :R], own_ref[:, R:], sib_ref[:, R:])


def solve_level(own, sibling, rest):
    wide = own.shape[1] - R
    params = pltpu.CompilerParams(vmem_limit_bytes=VMEM_BYTES)
    coeff = jax.ShapeDtypeStruct((R, wide), F32)
    if rest.shape[0] == 0:
        return pl.pallas_call(last_kernel, out_shape=coeff, compiler_params=params)(own, sibling), rest
    return pl.pallas_call(
        level_kernel,
        out_shape=(coeff, jax.ShapeDtypeStruct((rest.shape[0], wide), F32)),
        compiler_params=params,
    )(own, sibling, rest)


def finish_kernel(count, *refs):
    cols_ref, coeff_refs, block_refs = refs[0], refs[1 : 1 + LEVELS], refs[1 + LEVELS : -2]
    out_ref, hold_ref = refs[-2], refs[-1]
    width = R // count
    me = lax.axis_index("cols")
    finals = [ref[:, -TGT_PAD:] for ref in coeff_refs]
    for late in range(LEVELS - 1, 0, -1):
        for early in range(late):
            at = (late - early - 1) * R
            finals[early] -= mul(coeff_refs[early][:, at : at + R], finals[late])
    for level in range(LEVELS):
        hold_ref[level] = finals[level]
    total = cols_ref[:, :TGT_PAD]
    for apart in range(count):
        source = lax.rem(me - apart + count, count)
        block = block_refs[apart][...]
        at = pl.ds(pl.multiple_of(source * width, 8), width)
        parts = [hold_ref[level, at, :] for level in range(LEVELS - 1, -1, -1)]
        if block.shape[1] > LEVELS * width:
            parts.append(jnp.zeros((block.shape[1] - LEVELS * width, TGT_PAD), F32))
        total -= mul(block, jnp.concatenate(parts, axis=0))
    out_ref[...] = total[:, :TGT_DEV]


def finish(count, columns, coeffs, blocks):
    return pl.pallas_call(
        functools.partial(finish_kernel, count),
        out_shape=jax.ShapeDtypeStruct((columns.shape[0], TGT_DEV), F32),
        scratch_shapes=[pltpu.VMEM((LEVELS, R, TGT_PAD), F32)],
        compiler_params=pltpu.CompilerParams(vmem_limit_bytes=VMEM_BYTES),
    )(columns, *coeffs, *blocks)


def partner(block, step, count):
    return lax.ppermute(block, "rows", [(i, i ^ 1 << step) for i in range(count)])


def around(block, count):
    return [block] + [
        lax.ppermute(block, "cols", [(i, (i + apart) % count) for i in range(count)])
        for apart in range(1, count)
    ]


def on_device(columns, row_bases, order):
    rows_dev = columns.shape[0]
    row_count = lax.axis_size("rows")
    col_count = lax.axis_size("cols")
    depth = row_count.bit_length() - 1
    bits = [depth - LEVELS + level for level in range(LEVELS)]
    scales = [0.55 / math.sqrt(R * rows_dev * (1 << bit)) for bit in bits]
    basis = columns[:, TGT_DEV:]
    if basis.shape[1] < LANES:
        basis = jnp.pad(basis, ((0, 0), (0, LANES - basis.shape[1])))
    tgt, own_basis = project(scales, columns, basis, row_bases, order)
    rest = jnp.concatenate([assemble(col_count, around(own_basis, col_count)), tgt], axis=1)
    blocks = around(basis, col_count)
    coeffs = []
    for level in range(LEVELS):
        own, rest = rest[:R], rest[R:]
        for step in range(bits[level]):
            own = own + partner(own, step, row_count)
        sibling = partner(own, bits[level], row_count)
        coeff, rest = solve_level(own, sibling, rest)
        coeffs.append(coeff)
    return finish(col_count, columns, coeffs, blocks)


def solution(mesh):
    placed = (P("rows", "cols"), P(None, "rows", None), P("rows", None))
    return jax.shard_map(
        on_device, mesh=mesh, in_specs=placed, out_specs=P("rows", "cols"), check_vma=False
    )
```

time: 418 us -> 140 us (0.33); the launches traced: 413 us -> 140 us
  other arithmetic: 223 us -> 0.36 us
  blocking collectives: 71 us -> 0 us
  Pallas kernels: 0 us -> 52.1 us
  waiting for transfers between devices: 23.4 us -> 64.9 us
  matrix products: 38 us -> 0 us
  local copies, waits for them, and re-layouts: 41.7 us -> 6.26 us
  starting transfers between devices: 8.32 us -> 16.4 us
  between operations: 6.02 us -> 0.17 us
    another operation x36 -> x0, other arithmetic: 217 us -> none  [the longest x27 138 us: solve_system(): factor = jnp.linalg.cholesky(gram)]
    all_gather x12 -> x0, blocking collectives: 71 us -> none  [the longest x4 32.6 us: on_device(): lax.all_gather(tree[:, start:start + width_block], 'cols', axis=1, tiled=...]
    pallas_call x0 -> x7, Pallas kernels: none -> 52.1 us  [the longest x3 28.5 us: solve_level(): pl.pallas_call(level_kernel, out_shape=(coeff, jax.ShapeDtypeStruct((rest...]
    ppermute x10 -> x12, waiting for transfers between devices: 23.4 us -> 64.9 us  [the longest x10 53 us: partner(): lax.ppermute(block, 'rows', [(i, i ^ 1 << step) for i in range(count)])]
    dot_general x16 -> x0, matrix products: 23.4 us -> none  [the longest x4 11.7 us: on_device(): jnp.einsum('cr,cq->rq', feats, tree[:, :start + width_block], precision=H...]
    another operation x35 -> x0, local copies, waits for them, and re-layouts: 15.9 us -> none
    another operation x32 -> x0, matrix products: 14.6 us -> none  [the longest x12 6.58 us: solve_system(): lax.linalg.triangular_solve(factor, middle, left_side=True, lower=True, t...]
    gather x2 -> x0, local copies, waits for them, and re-layouts: 8.35 us -> none  [on_device(): tree = jnp.take(columns, places, axis=0)]
  transfers between devices with their start and end apart: 10 -> 12, of which waited for: 6 -> 10; matrix products, arithmetic and copies ran while one was open for 0% -> 0% of each run, Pallas kernels for 0% -> 6%
where the time goes in v1:
time: 140 us
  waiting for transfers between devices  64.9 us (46%)
  Pallas kernels  52.1 us (37%)
  starting transfers between devices  16.4 us (12%)
  local copies, waits for them, and re-layouts  6.26 us (4%)
    ppermute x10, waiting for transfers between devices, partner(): lax.ppermute(block, 'rows', [(i, i ^ 1 << step) for i in range(count)])  53 us
    pallas_call x3, Pallas kernels, solve_level(): pl.pallas_call(level_kernel, out_shape=(coeff, jax.ShapeDtypeStruct((rest...  28.5 us
    ppermute x2, waiting for transfers between devices, around(): lax.ppermute(block, 'cols', [(i, (i + apart) % count) for i in range(coun...  11.9 us
    ppermute x10, starting transfers between devices, partner(): lax.ppermute(block, 'rows', [(i, i ^ 1 << step) for i in range(count)])  11.6 us
    pallas_call x1, Pallas kernels, project(): pl.pallas_call(functools.partial(project_kernel, scales), out_shape=(jax....  9.45 us
    pallas_call x1, Pallas kernels, solve_level(): pl.pallas_call(last_kernel, out_shape=coeff, compiler_params=params)  8.85 us
    ppermute x2, starting transfers between devices, around(): lax.ppermute(block, 'cols', [(i, (i + apart) % count) for i in range(coun...  4.79 us
    pallas_call x1, Pallas kernels, finish(): pl.pallas_call(functools.partial(finish_kernel, count), out_shape=jax.Sha...  4.62 us
  transfers between devices with their start and end apart: 12, of which 10 were waited for; matrix products, arithmetic and copies ran while one was open for 0% of the time, Pallas kernels for 6%

profile of v1, /device:TPU:0, one launch (start us, length us, event | category | flops | bytes accessed | tf_op | source)
XLA Modules:
  0.0 140.2 jit_solution(1857700961901339242)
XLA Ops:
  0.0 0.0 copy-start.1
  0.0 2.1 %copy.6.cols_ref.refs_0_ = f32[1024,576]{1,0:T(8,128)S(1)} copy(f32[1024,576]{0,1:T(8,128)} %param.3) | data formatting | bytes 4718592 | tf_op args[0]
  2.1 0.0 copy-start.2
  2.1 0.0 copy-start
  2.1 0.3 slice.28.basis_ref.refs_5_
  2.5 1.1 copy-done.2
  3.6 0.0 copy-done.1
  3.6 1.0 copy-done
  4.7 9.5 %shard_map.37 = (f32[512,384]{1,0:T(8,128)S(1)}, f32[512,256]{1,0:T(8,128)S(1)}) custom-call(f32[1024,576]{1,0:T(8,128)} %copy-done.2, f32[1024,256]{1,0:T(8,128)S(1)} %slice.28.basis_ref.refs_5_, f32[4,1024,128]{2,1,0:T(8,128)S(1)} %copy-done, s32[1,1024]{1,0:T(1,128)S(1)} %copy-done.1), custom_call_target="tpu_custom_call" | custom-call | tf_op jit(solution)/shard_map/pallas_call | solution.py:151
  14.1 3.0 %collective-permute-start = (f32[512,256]{1,0:T(8,128)S(1)}, f32[512,256]{1,0:T(8,128)S(1)}, u32[]{:S(2)}, u32[]{:S(2)}) collective-permute-start(f32[512,256]{1,0:T(8,128)S(1)} %get-tuple-element.13.refs_0_), channel_id=1, source_target_pairs={{0,1},{1,0},{2,3},{3,2},{4,5},{5,4},{6,7},{7,6},{8,9},{9,8},{10,11... | collective-permute-start | bytes 1572872 | tf_op jit(solution)/shard_map/ppermute | solution.py:251
  17.2 11.9 %collective-permute-done.refs_1_ = f32[512,256]{1,0:T(8,128)S(1)} collective-permute-done((f32[512,256]{1,0:T(8,128)S(1)}, f32[512,256]{1,0:T(8,128)S(1)}, u32[]{:S(2)}, u32[]{:S(2)}) %collective-permute-start) | collective-permute-done | bytes 524320 | tf_op jit(solution)/shard_map/ppermute | solution.py:251
  29.1 0.6 shard_map.38
  29.8 0.1 collective-permute-start.1
  29.8 0.1 pad_maximum_fusion.rest_ref
  29.9 1.7 %collective-permute-done.1.sib_ref = f32[128,896]{1,0:T(8,128)S(1)} collective-permute-done((f32[128,896]{1,0:T(8,128)S(1)}, f32[128,896]{1,0:T(8,128)S(1)}, u32[]{:S(2)}, u32[]{:S(2)}) %collective-permute-start.1) | collective-permute-done | bytes 458784 | tf_op jit(solution)/shard_map/ppermute | solution.py:246
  31.6 9.7 %shard_map.39 = (f32[128,768]{1,0:T(8,128)S(1)}, f32[384,768]{1,0:T(8,128)S(1)}) custom-call(f32[128,896]{1,0:T(8,128)S(1)} %pad_maximum_fusion.1.own_ref, f32[128,896]{1,0:T(8,128)S(1)} %collective-permute-done.1.sib_ref, f32[384,896]{1,0:T(8,128)S(1)} %pad_maximum_fusion.rest_ref), custom_call_target="tpu_custom_call" | custom-call | tf_op jit(solution)/shard_map/pallas_call | solution.py:205
  41.3 0.2 collective-permute-start.2
  41.5 1.6 %collective-permute-done.2 = f32[128,768]{1,0:T(8,128)S(1)} collective-permute-done((f32[128,768]{1,0:T(8,128)S(1)}, f32[128,768]{1,0:T(8,128)S(1)}, u32[]{:S(2)}, u32[]{:S(2)}) %collective-permute-start.2) | collective-permute-done | bytes 393248 | tf_op jit(solution)/shard_map/ppermute | solution.py:246
  43.2 1.8 %collective-permute-start.3 = (f32[128,768]{1,0:T(8,128)S(1)}, f32[128,768]{1,0:T(8,128)S(1)}, u32[]{:S(2)}, u32[]{:S(2)}) collective-permute-start(f32[128,768]{1,0:T(8,128)S(1)} %slice_add_fusion.1.own_ref), channel_id=1, source_target_pairs={{0,4},{2,6},{4,0},{6,2},{8,12},{10,14},{12,8},{14,10},{16,20},{18,... | collective-permute-start | bytes 1179656 | tf_op jit(solution)/shard_map/ppermute | solution.py:246
  45.0 0.1 slice.25.rest_ref
  45.0 9.4 %collective-permute-done.3.sib_ref = f32[128,768]{1,0:T(8,128)S(1)} collective-permute-done((f32[128,768]{1,0:T(8,128)S(1)}, f32[128,768]{1,0:T(8,128)S(1)}, u32[]{:S(2)}, u32[]{:S(2)}) %collective-permute-start.3) | collective-permute-done | bytes 393248 | tf_op jit(solution)/shard_map/ppermute | solution.py:246
  54.4 9.4 %shard_map.40 = (f32[128,640]{1,0:T(8,128)S(1)}, f32[256,640]{1,0:T(8,128)S(1)}) custom-call(f32[128,768]{1,0:T(8,128)S(1)} %slice_add_fusion.1.own_ref, f32[128,768]{1,0:T(8,128)S(1)} %collective-permute-done.3.sib_ref, f32[256,768]{1,0:T(8,128)S(1)} %slice.25.rest_ref), custom_call_target="tpu_custom_call" | custom-call | tf_op jit(solution)/shard_map/pallas_call | solution.py:205
  63.9 0.1 collective-permute-start.4
  64.0 1.6 %collective-permute-done.4 = f32[128,640]{1,0:T(8,128)S(1)} collective-permute-done((f32[128,640]{1,0:T(8,128)S(1)}, f32[128,640]{1,0:T(8,128)S(1)}, u32[]{:S(2)}, u32[]{:S(2)}) %collective-permute-start.4) | collective-permute-done | bytes 327712 | tf_op jit(solution)/shard_map/ppermute | solution.py:246
  65.6 0.1 fusion
  65.6 1.8 %collective-permute-start.5 = (f32[128,640]{1,0:T(8,128)S(1)}, f32[128,640]{1,0:T(8,128)S(1)}, u32[]{:S(2)}, u32[]{:S(2)}) collective-permute-start(f32[128,640]{1,0:T(8,128)S(1)} %get-tuple-element.22), channel_id=1, source_target_pairs={{0,4},{2,6},{4,0},{6,2},{8,12},{10,14},{12,8},{14,10},{16,20},{18,... | collective-permute-start | bytes 983048 | tf_op jit(solution)/shard_map/ppermute | solution.py:246
  67.4 8.0 %collective-permute-done.5 = f32[128,640]{1,0:T(8,128)S(1)} collective-permute-done((f32[128,640]{1,0:T(8,128)S(1)}, f32[128,640]{1,0:T(8,128)S(1)}, u32[]{:S(2)}, u32[]{:S(2)}) %collective-permute-start.5) | collective-permute-done | bytes 327712 | tf_op jit(solution)/shard_map/ppermute | solution.py:246
  75.5 1.9 %collective-permute-start.6 = (f32[128,640]{1,0:T(8,128)S(1)}, f32[128,640]{1,0:T(8,128)S(1)}, u32[]{:S(2)}, u32[]{:S(2)}) collective-permute-start(f32[128,640]{1,0:T(8,128)S(1)} %add.20.own_ref), channel_id=1, source_target_pairs={{0,8},{2,10},{4,12},{6,14},{8,0},{10,2},{12,4},{14,6},{16,24},{18,... | collective-permute-start | bytes 983048 | tf_op jit(solution)/shard_map/ppermute | solution.py:246
  77.4 7.2 %collective-permute-done.6.sib_ref = f32[128,640]{1,0:T(8,128)S(1)} collective-permute-done((f32[128,640]{1,0:T(8,128)S(1)}, f32[128,640]{1,0:T(8,128)S(1)}, u32[]{:S(2)}, u32[]{:S(2)}) %collective-permute-start.6) | collective-permute-done | bytes 327712 | tf_op jit(solution)/shard_map/ppermute | solution.py:246
  84.5 9.4 %shard_map.41 = (f32[128,512]{1,0:T(8,128)S(1)}, f32[128,512]{1,0:T(8,128)S(1)}) custom-call(f32[128,640]{1,0:T(8,128)S(1)} %add.20.own_ref, f32[128,640]{1,0:T(8,128)S(1)} %collective-permute-done.6.sib_ref, f32[128,640]{1,0:T(8,128)S(1)} %get-tuple-element.21.rest_ref), custom_call_target="tpu_custom_call" | custom-call | tf_op jit(solution)/shard_map/pallas_call | solution.py:205
  94.0 0.1 collective-permute-start.7
  94.0 1.8 %collective-permute-start.11 = (f32[1024,256]{1,0:T(8,128)S(1)}, f32[1024,256]{1,0:T(8,128)S(1)}, u32[]{:S(2)}, u32[]{:S(2)}) collective-permute-start(f32[1024,256]{1,0:T(8,128)S(1)} %slice.28.basis_ref.refs_5_), channel_id=1, source_target_pairs={{0,1},{1,0},{2,3},{3,2},{4,5},{5,4},{6,7},{7,6},{8,9},{9,8},{10,11... | collective-permute-start | bytes 3145736 | tf_op jit(solution)/shard_map/ppermute | solution.py:251
  95.8 0.0 collective-permute-done.7
  95.8 1.5 %collective-permute-start.8 = (f32[128,512]{1,0:T(8,128)S(1)}, f32[128,512]{1,0:T(8,128)S(1)}, u32[]{:S(2)}, u32[]{:S(2)}) collective-permute-start(f32[128,512]{1,0:T(8,128)S(1)} %add.21), channel_id=1, source_target_pairs={{0,4},{2,6},{4,0},{6,2},{8,12},{10,14},{12,8},{14,10},{16,20},{18,... | collective-permute-start | bytes 786440 | tf_op jit(solution)/shard_map/ppermute | solution.py:246
  97.4 6.9 %collective-permute-done.8 = f32[128,512]{1,0:T(8,128)S(1)} collective-permute-done((f32[128,512]{1,0:T(8,128)S(1)}, f32[128,512]{1,0:T(8,128)S(1)}, u32[]{:S(2)}, u32[]{:S(2)}) %collective-permute-start.8) | collective-permute-done | bytes 262176 | tf_op jit(solution)/shard_map/ppermute | solution.py:246
  104.3 1.6 %collective-permute-start.9 = (f32[128,512]{1,0:T(8,128)S(1)}, f32[128,512]{1,0:T(8,128)S(1)}, u32[]{:S(2)}, u32[]{:S(2)}) collective-permute-start(f32[128,512]{1,0:T(8,128)S(1)} %add.22), channel_id=1, source_target_pairs={{0,8},{2,10},{4,12},{6,14},{8,0},{10,2},{12,4},{14,6},{16,24},{18,... | collective-permute-start | bytes 786440 | tf_op jit(solution)/shard_map/ppermute | solution.py:246
  105.9 6.0 %collective-permute-done.9 = f32[128,512]{1,0:T(8,128)S(1)} collective-permute-done((f32[128,512]{1,0:T(8,128)S(1)}, f32[128,512]{1,0:T(8,128)S(1)}, u32[]{:S(2)}, u32[]{:S(2)}) %collective-permute-start.9) | collective-permute-done | bytes 262176 | tf_op jit(solution)/shard_map/ppermute | solution.py:246
  112.0 2.6 %collective-permute-start.10 = (f32[128,512]{1,0:T(8,128)S(1)}, f32[128,512]{1,0:T(8,128)S(1)}, u32[]{:S(2)}, u32[]{:S(2)}) collective-permute-start(f32[128,512]{1,0:T(8,128)S(1)} %add.23.own_ref), channel_id=1, source_target_pairs={{0,16},{2,18},{4,20},{6,22},{8,24},{10,26},{12,28},{14,30},{16,0},... | collective-permute-start | bytes 786440 | tf_op jit(solution)/shard_map/ppermute | solution.py:246
  114.6 10.6 %collective-permute-done.10.sib_ref = f32[128,512]{1,0:T(8,128)S(1)} collective-permute-done((f32[128,512]{1,0:T(8,128)S(1)}, f32[128,512]{1,0:T(8,128)S(1)}, u32[]{:S(2)}, u32[]{:S(2)}) %collective-permute-start.10) | collective-permute-done | bytes 262176 | tf_op jit(solution)/shard_map/ppermute | solution.py:246
  125.2 8.9 %shard_map.42.refs_4_ = f32[128,384]{1,0:T(8,128)S(1)} custom-call(f32[128,512]{1,0:T(8,128)S(1)} %add.23.own_ref, f32[128,512]{1,0:T(8,128)S(1)} %collective-permute-done.10.sib_ref), custom_call_target="tpu_custom_call" | custom-call | tf_op jit(solution)/shard_map/pallas_call | solution.py:204
  134.0 0.0 collective-permute-done.11.refs_6_
  134.0 4.6 %shard_map.43 = f32[1024,320]{1,0:T(8,128)S(1)} custom-call(f32[1024,576]{1,0:T(8,128)} %copy-done.2, f32[128,768]{1,0:T(8,128)S(1)} %get-tuple-element.15.refs_1_, f32[128,640]{1,0:T(8,128)S(1)} %get-tuple-element.17.refs_2_, f32[128,512]{1,0:T(8,128)S(1)} %get-tuple-element.19.refs_3_, f32[128,384]{1,0:T(8,128)S(1)} %shard_map.42.refs_4_, ...), custom_call_target="tpu_custom_call" | custom-call | tf_op jit(solution)/shard_map/pallas_call | solution.py:237
  138.7 1.5 %copy.7 = f32[1024,320]{0,1:T(8,128)} copy(f32[1024,320]{1,0:T(8,128)S(1)} %shard_map.43) | data formatting | bytes 2621440 | tf_op jit(solution)/shard_map/pallas_call | solution.py:237
  (8 shorter events, 0.3 us)
Async XLA Ops:
  0.0 3.6 %copy-start.1 = (s32[1,1024]{1,0:T(1,128)S(1)}, s32[1,1024]{1,0:T(1,128)}, u32[]{:S(2)}) copy-start(s32[1,1024]{1,0:T(1,128)} %order_ref.1) | copy-start | bytes 12292
  2.1 1.5 %copy-start.2 = (f32[1024,576]{1,0:T(8,128)}, f32[1024,576]{1,0:T(8,128)S(1)}, u32[]{:S(2)}) copy-start(f32[1024,576]{1,0:T(8,128)S(1)} %copy.6.cols_ref.refs_0_) | copy-start | bytes 7077892
  2.1 2.5 %copy-start = (f32[4,1024,128]{2,1,0:T(8,128)S(1)}, f32[4,1024,128]{2,1,0:T(8,128)}, u32[]{:S(2)}) copy-start(f32[4,1024,128]{2,1,0:T(8,128)} %bases_ref.1) | copy-start | bytes 6291460
  14.1 15.0 %collective-permute-start = (f32[512,256]{1,0:T(8,128)S(1)}, f32[512,256]{1,0:T(8,128)S(1)}, u32[]{:S(2)}, u32[]{:S(2)}) collective-permute-start(f32[512,256]{1,0:T(8,128)S(1)} %get-tuple-element.13.refs_0_), channel_id=1, source_target_pairs={{0,1},{1,0},{2,3},{3,2},{4,5},{5,4},{6,7},{7,6},{8,9},{9,8},{10,11... | collective-permute-start | bytes 1572872 | tf_op jit(solution)/shard_map/ppermute | solution.py:251
  29.8 1.9 %collective-permute-start.1 = (f32[128,896]{1,0:T(8,128)S(1)}, f32[128,896]{1,0:T(8,128)S(1)}, u32[]{:S(2)}, u32[]{:S(2)}) collective-permute-start(f32[128,896]{1,0:T(8,128)S(1)} %pad_maximum_fusion.1.own_ref), channel_id=1, source_target_pairs={{0,2},{2,0},{4,6},{6,4},{8,10},{10,8},{12,14},{14,12},{16,18},{18,... | collective-permute-start | bytes 1376264 | tf_op jit(solution)/shard_map/ppermute | solution.py:246
  41.3 1.8 %collective-permute-start.2 = (f32[128,768]{1,0:T(8,128)S(1)}, f32[128,768]{1,0:T(8,128)S(1)}, u32[]{:S(2)}, u32[]{:S(2)}) collective-permute-start(f32[128,768]{1,0:T(8,128)S(1)} %slice.24), channel_id=1, source_target_pairs={{0,2},{2,0},{4,6},{6,4},{8,10},{10,8},{12,14},{14,12},{16,18},{18,... | collective-permute-start | bytes 1179656 | tf_op jit(solution)/shard_map/ppermute | solution.py:246
  43.2 11.2 %collective-permute-start.3 = (f32[128,768]{1,0:T(8,128)S(1)}, f32[128,768]{1,0:T(8,128)S(1)}, u32[]{:S(2)}, u32[]{:S(2)}) collective-permute-start(f32[128,768]{1,0:T(8,128)S(1)} %slice_add_fusion.1.own_ref), channel_id=1, source_target_pairs={{0,4},{2,6},{4,0},{6,2},{8,12},{10,14},{12,8},{14,10},{16,20},{18,... | collective-permute-start | bytes 1179656 | tf_op jit(solution)/shard_map/ppermute | solution.py:246
  63.9 1.7 %collective-permute-start.4 = (f32[128,640]{1,0:T(8,128)S(1)}, f32[128,640]{1,0:T(8,128)S(1)}, u32[]{:S(2)}, u32[]{:S(2)}) collective-permute-start(f32[128,640]{1,0:T(8,128)S(1)} %slice.26), channel_id=1, source_target_pairs={{0,2},{2,0},{4,6},{6,4},{8,10},{10,8},{12,14},{14,12},{16,18},{18,... | collective-permute-start | bytes 983048 | tf_op jit(solution)/shard_map/ppermute | solution.py:246
  65.6 9.8 %collective-permute-start.5 = (f32[128,640]{1,0:T(8,128)S(1)}, f32[128,640]{1,0:T(8,128)S(1)}, u32[]{:S(2)}, u32[]{:S(2)}) collective-permute-start(f32[128,640]{1,0:T(8,128)S(1)} %get-tuple-element.22), channel_id=1, source_target_pairs={{0,4},{2,6},{4,0},{6,2},{8,12},{10,14},{12,8},{14,10},{16,20},{18,... | collective-permute-start | bytes 983048 | tf_op jit(solution)/shard_map/ppermute | solution.py:246
  75.5 9.0 %collective-permute-start.6 = (f32[128,640]{1,0:T(8,128)S(1)}, f32[128,640]{1,0:T(8,128)S(1)}, u32[]{:S(2)}, u32[]{:S(2)}) collective-permute-start(f32[128,640]{1,0:T(8,128)S(1)} %add.20.own_ref), channel_id=1, source_target_pairs={{0,8},{2,10},{4,12},{6,14},{8,0},{10,2},{12,4},{14,6},{16,24},{18,... | collective-permute-start | bytes 983048 | tf_op jit(solution)/shard_map/ppermute | solution.py:246
  94.0 1.8 %collective-permute-start.7 = (f32[128,512]{1,0:T(8,128)S(1)}, f32[128,512]{1,0:T(8,128)S(1)}, u32[]{:S(2)}, u32[]{:S(2)}) collective-permute-start(f32[128,512]{1,0:T(8,128)S(1)} %get-tuple-element.20), channel_id=1, source_target_pairs={{0,2},{2,0},{4,6},{6,4},{8,10},{10,8},{12,14},{14,12},{16,18},{18,... | collective-permute-start | bytes 786440 | tf_op jit(solution)/shard_map/ppermute | solution.py:246
  94.0 40.0 %collective-permute-start.11 = (f32[1024,256]{1,0:T(8,128)S(1)}, f32[1024,256]{1,0:T(8,128)S(1)}, u32[]{:S(2)}, u32[]{:S(2)}) collective-permute-start(f32[1024,256]{1,0:T(8,128)S(1)} %slice.28.basis_ref.refs_5_), channel_id=1, source_target_pairs={{0,1},{1,0},{2,3},{3,2},{4,5},{5,4},{6,7},{7,6},{8,9},{9,8},{10,11... | collective-permute-start | bytes 3145736 | tf_op jit(solution)/shard_map/ppermute | solution.py:251
  95.8 8.4 %collective-permute-start.8 = (f32[128,512]{1,0:T(8,128)S(1)}, f32[128,512]{1,0:T(8,128)S(1)}, u32[]{:S(2)}, u32[]{:S(2)}) collective-permute-start(f32[128,512]{1,0:T(8,128)S(1)} %add.21), channel_id=1, source_target_pairs={{0,4},{2,6},{4,0},{6,2},{8,12},{10,14},{12,8},{14,10},{16,20},{18,... | collective-permute-start | bytes 786440 | tf_op jit(solution)/shard_map/ppermute | solution.py:246
  104.3 7.6 %collective-permute-start.9 = (f32[128,512]{1,0:T(8,128)S(1)}, f32[128,512]{1,0:T(8,128)S(1)}, u32[]{:S(2)}, u32[]{:S(2)}) collective-permute-start(f32[128,512]{1,0:T(8,128)S(1)} %add.22), channel_id=1, source_target_pairs={{0,8},{2,10},{4,12},{6,14},{8,0},{10,2},{12,4},{14,6},{16,24},{18,... | collective-permute-start | bytes 786440 | tf_op jit(solution)/shard_map/ppermute | solution.py:246
  112.0 13.2 %collective-permute-start.10 = (f32[128,512]{1,0:T(8,128)S(1)}, f32[128,512]{1,0:T(8,128)S(1)}, u32[]{:S(2)}, u32[]{:S(2)}) collective-permute-start(f32[128,512]{1,0:T(8,128)S(1)} %add.23.own_ref), channel_id=1, source_target_pairs={{0,16},{2,18},{4,20},{6,22},{8,24},{10,26},{12,28},{14,30},{16,0},... | collective-permute-start | bytes 786440 | tf_op jit(solution)/shard_map/ppermute | solution.py:246

commit v2 on v1

v2 whole, which is shorter than its diff:
```python
import functools
import math

import jax
import jax.numpy as jnp
from jax import lax
from jax.experimental import pallas as pl
from jax.experimental.pallas import tpu as pltpu
from jax.sharding import PartitionSpec as P

R = 128
LEVELS = 4
TGT_DEV = 320
LANES = 128
TGT_PAD = -(-TGT_DEV // LANES) * LANES
VMEM_BYTES = 48 * 1024 * 1024
F32 = jnp.float32
BF16 = jnp.bfloat16

ROWS_ON_COLS = (((1,), (0,)), ((), ()))
COLS_ON_COLS = (((0,), (0,)), ((), ()))


def halves(value):
    high = value.astype(BF16)
    return high, (value - high.astype(F32)).astype(BF16)


def mul_halves(left, right, dims=ROWS_ON_COLS):
    def one(a, b):
        return lax.dot_general(a, b, dims, preferred_element_type=F32)

    return one(left[0], right[0]) + (one(left[0], right[1]) + one(left[1], right[0]))


def mul(left, right):
    return mul_halves(halves(left), halves(right))


def mul_full(left, right, dims=ROWS_ON_COLS):
    return lax.dot_general(
        left, right, dims, precision=lax.Precision.HIGHEST, preferred_element_type=F32
    )


def invert_two(a, b, d):
    ia = 1.0 / a
    t = b * ia
    low = 1.0 / (d - b * t)
    mid = -t * low
    return ia - t * mid, mid, low


def invert_four(d):
    e00, e01, e11 = invert_two(d[0][0], d[0][1], d[1][1])
    f00, f01, f10, f11 = d[0][2], d[0][3], d[1][2], d[1][3]
    w00, w01 = e00 * f00 + e01 * f10, e00 * f01 + e01 * f11
    w10, w11 = e01 * f00 + e11 * f10, e01 * f01 + e11 * f11
    s00 = d[2][2] - (f00 * w00 + f10 * w10)
    s01 = d[2][3] - (f00 * w01 + f10 * w11)
    s11 = d[3][3] - (f01 * w01 + f11 * w11)
    g00, g01, g11 = invert_two(s00, s01, s11)
    u00, u01 = w00 * g00 + w01 * g01, w00 * g01 + w01 * g11
    u10, u11 = w10 * g00 + w11 * g01, w10 * g01 + w11 * g11
    t00 = e00 + u00 * w00 + u01 * w01
    t01 = e01 + u00 * w10 + u01 * w11
    t11 = e11 + u10 * w10 + u11 * w11
    return [
        [t00, t01, -u00, -u01],
        [t01, t11, -u10, -u11],
        [-u00, -u10, g00, g01],
        [-u01, -u11, g01, g11],
    ]


def sweep_four(tiles, first):
    lane = lax.broadcasted_iota(jnp.int32, (8, LANES), 1)
    sub = lax.broadcasted_iota(jnp.int32, (8, LANES), 0)
    spread = [
        [jnp.broadcast_to(tile[:, first + j : first + j + 1], (8, LANES)) for j in range(4)]
        for tile in tiles
    ]
    pivot = [
        [jnp.broadcast_to(spread[0][j][first + i : first + i + 1], (8, LANES)) for j in range(4)]
        for i in range(4)
    ]
    inverse = invert_four(pivot)
    rows = [
        jnp.where(
            (lane >= first) & (lane < first + 4),
            jnp.where(lane == first + j, 1.0, 0.0),
            jnp.broadcast_to(tiles[0][first + j : first + j + 1], (8, LANES)),
        )
        for j in range(4)
    ]
    solved = [
        (inverse[i][0] * rows[0] + inverse[i][1] * rows[1])
        + (inverse[i][2] * rows[2] + inverse[i][3] * rows[3])
        for i in range(4)
    ]
    kept = (lane < first) | (lane >= first + 4)
    out = []
    for tile, cols in zip(tiles, spread):
        change = (cols[0] * solved[0] + cols[1] * solved[1]) + (
            cols[2] * solved[2] + cols[3] * solved[3]
        )
        out.append(jnp.where(kept, tile, 0.0) - change)
    for i in range(4):
        out[0] = jnp.where(sub == first + i, solved[i], out[0])
    return out


def invert_spd(gram, between):
    count = R // 8

    def body(_, tiles):
        tiles = sweep_four(list(tiles), 0)
        tiles = sweep_four(tiles, 4)
        tiles = tiles[1:] + tiles[:1]
        return tuple(pltpu.roll(tile, LANES - 8, 1) for tile in tiles)

    tiles = tuple(gram[8 * i : 8 * i + 8] for i in range(count))
    parts = len(between) + 1
    for part in range(parts):
        tiles = lax.fori_loop(count * part // parts, count * (part + 1) // parts, body, tiles)
        if part < len(between):
            between[part]()
    return jnp.concatenate(tiles, axis=0)


def project_kernel(scales, cols_ref, bases_ref, order_ref, tgt_ref, own_ref):
    rows = cols_ref.shape[1]
    place = lax.broadcasted_iota(jnp.int32, (rows, rows), 0)
    pick = jnp.where(place == order_ref[...], 1.0, 0.0).astype(BF16)
    cols = halves(cols_ref[...])
    for level in range(LEVELS):
        high, low = halves(bases_ref[level])
        high = jnp.dot(pick, high, preferred_element_type=F32).astype(BF16)
        low = jnp.dot(pick, low, preferred_element_type=F32).astype(BF16)
        at = pl.ds(level * R, R)
        found = scales[level] * mul_halves(cols, (high, low))
        tgt_ref[at, :] = found[:TGT_PAD].T
        basis = found[TGT_DEV:]
        if basis.shape[0] < LANES:
            short = LANES - basis.shape[0]
            basis = jnp.concatenate([basis, jnp.zeros((short, R), F32)], axis=0)
        own_ref[at, :] = basis.T


def project(scales, columns, row_bases, order):
    return pl.pallas_call(
        functools.partial(project_kernel, scales),
        out_shape=(
            jax.ShapeDtypeStruct((LEVELS * R, TGT_PAD), F32),
            jax.ShapeDtypeStruct((LEVELS * R, max(columns.shape[0] - TGT_DEV, LANES)), F32),
        ),
        compiler_params=pltpu.CompilerParams(vmem_limit_bytes=VMEM_BYTES),
    )(columns, row_bases, order)


def spread_level(block, level, width, source):
    offset = (LEVELS - 1 - level) * width
    tile = block[:, offset // LANES * LANES : offset // LANES * LANES + LANES]
    shift = lax.rem(source * width - offset % LANES + LANES, LANES)
    lane = lax.broadcasted_iota(jnp.int32, tile.shape, 1)
    inside = (lane >= source * width) & (lane < (source + 1) * width)
    return jnp.where(inside, pltpu.roll(tile, shift, 1), 0.0)


def sweep_kernel(row_count, col_count, bits, *refs):
    tgt_ref, own_ref, cols_ref, out_ref, blocks_ref = refs[:5]
    work, peers, mine, theirs, held, landed, own_all, sib_all = refs[5:13]
    peer_sems, block_sems, couple_sems, rest_sems, join_sems = refs[13:]
    row, col = lax.axis_index("rows"), lax.axis_index("cols")
    width, half, wide = R // col_count, R // 2, LEVELS * R + TGT_PAD
    core = lax.rem(row, 2)
    my_half = pl.ds(pl.multiple_of(core * half, half), half)
    other_half = pl.ds(pl.multiple_of((1 - core) * half, half), half)
    row_peers = []
    for step in range(row_count.bit_length() - 1):
        bit = lax.rem(row // (1 << step), 2)
        row_peers.append((row + (1 << step) * (1 - 2 * bit), col))
    col_peers = [(row, lax.rem(col + apart, col_count)) for apart in range(1, col_count)]

    def send(src, dst, sems, device):
        copy = pltpu.make_async_remote_copy(
            src_ref=src,
            dst_ref=dst,
            send_sem=sems.at[0],
            recv_sem=sems.at[1],
            device_id=device,
            device_id_type=pl.DeviceIdType.MESH,
        )
        copy.start()
        return copy

    barrier = pltpu.get_barrier_semaphore()
    for device in row_peers + col_peers:
        pl.semaphore_signal(
            barrier, inc=1, device_id=device, device_id_type=pl.DeviceIdType.MESH
        )
    pl.semaphore_wait(barrier, len(row_peers) + len(col_peers))

    def level_rows(level):
        return pl.ds(level * R, R)

    gathers = [
        [
            send(
                own_ref.at[level_rows(level)],
                peers.at[k, level_rows(level)],
                peer_sems.at[k, level],
                device,
            )
            for k, device in enumerate(col_peers)
        ]
        for level in range(LEVELS)
    ]

    def gather(level):
        at = level_rows(level)
        for copy in gathers[level]:
            copy.wait()
        blocks = [own_ref[at, :]] + [peers[k, at, :] for k in range(len(col_peers))]
        for which in range(LEVELS):
            total = None
            for apart, block in enumerate(blocks):
                source = lax.rem(col - apart + col_count, col_count)
                part = spread_level(block, which, width, source)
                total = part if total is None else total + part
            work[at, which * R : (which + 1) * R] = total

    work[:, LEVELS * R :] = tgt_ref[...]
    gather(0)
    block_copies = []
    for level in range(LEVELS):
        last = bits[level]
        at, rest = level_rows(level), wide - (level + 1) * R
        rest_cols = pl.ds((level + 1) * R, rest)

        def couple_send(step):
            return send(
                mine.at[level, step],
                theirs.at[level, step],
                couple_sems.at[level, step],
                row_peers[step],
            )

        mine[level, 0] = work[at, level * R : (level + 1) * R]
        copy = couple_send(0)
        if level > 0:
            before = pl.ds((level - 1) * R, R)
            below = pl.ds(level * R, (LEVELS - level) * R)
            work[below, rest_cols] -= mul(work[below, before], coeffs_rest)
        rest_copies = {}

        def rest_send(step, src):
            rest_copies[step] = send(
                src,
                landed.at[level, step, pl.ds(0, src.shape[0]), pl.ds(0, rest)],
                rest_sems.at[level, step],
                row_peers[step],
            )

        if last == 0:
            rest_send(0, work.at[at, rest_cols])
        else:
            rest_send(0, work.at[pl.ds(pl.multiple_of(level * R + (1 - core) * half, half), half), rest_cols])
        for step in range(last):
            copy.wait()
            mine[level, step + 1] = mine[level, step] + theirs[level, step]
            copy = couple_send(step + 1)
        copy.wait()
        own_couple, sib_couple = mine[level, last], theirs[level, last]

        def held_at(step):
            return held.at[level, step, :, pl.ds(0, rest)]

        def advance(step):
            rest_copies[step].wait()
            arrived = landed[level, step, pl.ds(0, half), pl.ds(0, rest)]
            if step == 0:
                rows = pl.ds(pl.multiple_of(level * R + core * half, half), half)
                held[level, 0, :, pl.ds(0, rest)] = work[rows, rest_cols] + arrived
            else:
                held[level, step, :, pl.ds(0, rest)] = (
                    held[level, step - 1, :, pl.ds(0, rest)] + arrived
                )
            rest_send(step + 1, held_at(step))

        joins = []

        def join():
            rest_copies[last].wait()
            ours = held_at(last - 1)
            arrived = landed.at[level, last, pl.ds(0, half), pl.ds(0, rest)]
            for k, (src, whole) in enumerate(((ours, own_all), (arrived, sib_all))):
                place = whole.at[level, my_half, pl.ds(0, rest)]
                joins.append(send(src, place, join_sems.at[level, k], row_peers[0]))
                whole[level, my_half, pl.ds(0, rest)] = src[...]

        between = [functools.partial(advance, step) for step in range(1, last)]
        if last > 0:
            advance(0)
            between.append(join)
        unit_row = lax.broadcasted_iota(jnp.int32, (R, R), 0)
        unit_col = lax.broadcasted_iota(jnp.int32, (R, R), 1)
        reduced = jnp.where(unit_row == unit_col, 1.0, 0.0) - mul_full(sib_couple, own_couple)
        inverse = invert_spd(mul_full(reduced, reduced, COLS_ON_COLS), between)
        apply = mul_full(inverse, reduced, (((1,), (1,)), ((), ())))
        if level == 0:
            for later in range(1, LEVELS):
                gather(later)
            for k, device in enumerate(col_peers):
                src = cols_ref.at[pl.ds(TGT_DEV, cols_ref.shape[0] - TGT_DEV)]
                block_copies.append(send(src, blocks_ref.at[k], block_sems.at[k], device))
        if last == 0:
            rest_copies[0].wait()
            own_proj = work[at, rest_cols]
            sib_proj = landed[level, 0, :, pl.ds(0, rest)]
        else:
            for copy in joins:
                copy.wait()
            own_proj = own_all[level, :, pl.ds(0, rest)]
            sib_proj = sib_all[level, :, pl.ds(0, rest)]

        def coeffs_of(lo, hi):
            right = sib_proj[:, lo:hi] - mul(sib_couple, own_proj[:, lo:hi])
            return mul_full(apply, right)

        if level < LEVELS - 1:
            first = coeffs_of(0, R)
            out_ref[at, :R] = first
            below = pl.ds((level + 1) * R, (LEVELS - level - 1) * R)
            work[below, (level + 1) * R : (level + 2) * R] -= mul(
                work[below, level * R : (level + 1) * R], first
            )
            coeffs_rest = coeffs_of(R, rest)
            out_ref[at, R:rest] = coeffs_rest
        else:
            out_ref[at, :rest] = coeffs_of(0, rest)
    for copy in block_copies:
        copy.wait()


def sweep(row_count, col_count, bits, tgt, own_basis, columns):
    wide, steps = LEVELS * R + TGT_PAD, row_count.bit_length() - 1
    others = max(col_count - 1, 1)
    vmem = pl.BlockSpec(memory_space=pltpu.VMEM)
    hbm = pl.BlockSpec(memory_space=pl.ANY)
    return pl.pallas_call(
        functools.partial(sweep_kernel, row_count, col_count, bits),
        out_shape=(
            jax.ShapeDtypeStruct((LEVELS * R, wide - R), F32),
            jax.ShapeDtypeStruct((others, columns.shape[0] - TGT_DEV, columns.shape[1]), F32),
        ),
        in_specs=[vmem, vmem, hbm],
        out_specs=(vmem, hbm),
        scratch_shapes=[
            pltpu.VMEM((LEVELS * R, wide), F32),
            pltpu.VMEM((others,) + own_basis.shape, F32),
            pltpu.VMEM((LEVELS, steps, R, R), F32),
            pltpu.VMEM((LEVELS, steps, R, R), F32),
            pltpu.VMEM((LEVELS, steps, R // 2, wide - R), F32),
            pltpu.VMEM((LEVELS, steps, R, wide - R), F32),
            pltpu.VMEM((LEVELS, R, wide - R), F32),
            pltpu.VMEM((LEVELS, R, wide - R), F32),
            pltpu.SemaphoreType.DMA((others, LEVELS, 2)),
            pltpu.SemaphoreType.DMA((others, 2)),
            pltpu.SemaphoreType.DMA((LEVELS, steps, 2)),
            pltpu.SemaphoreType.DMA((LEVELS, steps, 2)),
            pltpu.SemaphoreType.DMA((LEVELS, 2, 2)),
        ],
        compiler_params=pltpu.CompilerParams(
            collective_id=0, has_side_effects=True, vmem_limit_bytes=VMEM_BYTES
        ),
    )(tgt, own_basis, columns)


def finish_kernel(count, cols_ref, coeff_ref, blocks_ref, out_ref, hold_ref):
    width = R // count
    me = lax.axis_index("cols")

    def coeff(level, first, last):
        return coeff_ref[level * R : (level + 1) * R, first * R : last * R]

    tgt_tiles = TGT_PAD // R
    finals = [
        coeff(level, LEVELS - 1 - level, LEVELS - 1 - level + tgt_tiles) for level in range(LEVELS)
    ]
    for late in range(LEVELS - 1, 0, -1):
        for early in range(late):
            at = late - early - 1
            finals[early] -= mul(coeff(early, at, at + 1), finals[late])
    for level in range(LEVELS):
        hold_ref[level] = finals[level]
    total = cols_ref[:TGT_DEV]
    for apart in range(count):
        source = lax.rem(me - apart + count, count)
        block = cols_ref[TGT_DEV:] if apart == 0 else blocks_ref[apart - 1]
        at = pl.ds(pl.multiple_of(source * width, 8), width)
        parts = [hold_ref[level, at, :] for level in range(LEVELS - 1, -1, -1)]
        parts = jnp.concatenate(parts, axis=0).T[:TGT_DEV]
        total -= mul(parts, block)
    out_ref[...] = total


def finish(count, columns, coeffs, blocks):
    return pl.pallas_call(
        functools.partial(finish_kernel, count),
        out_shape=jax.ShapeDtypeStruct((TGT_DEV, columns.shape[1]), F32),
        scratch_shapes=[pltpu.VMEM((LEVELS, R, TGT_PAD), F32)],
        compiler_params=pltpu.CompilerParams(vmem_limit_bytes=VMEM_BYTES),
    )(columns, coeffs, blocks)


def on_device(columns, row_bases, order):
    rows_dev = columns.shape[0]
    row_count = lax.axis_size("rows")
    col_count = lax.axis_size("cols")
    depth = row_count.bit_length() - 1
    bits = [depth - LEVELS + level for level in range(LEVELS)]
    scales = [0.55 / math.sqrt(R * rows_dev * (1 << bit)) for bit in bits]
    columns = columns.T
    tgt, own_basis = project(scales, columns, row_bases, order)
    coeffs, blocks = sweep(row_count, col_count, bits, tgt, own_basis, columns)
    return finish(col_count, columns, coeffs, blocks).T


def solution(mesh):
    placed = (P("rows", "cols"), P(None, "rows", None), P("rows", None))
    return jax.shard_map(
        on_device, mesh=mesh, in_specs=placed, out_specs=P("rows", "cols"), check_vma=False
    )
```

time: 140 us -> 102 us (0.73)
  waiting for transfers between devices: 64.9 us -> 0 us
  Pallas kernels: 52.1 us -> 97.8 us
  starting transfers between devices: 16.4 us -> 0 us
  local copies, waits for them, and re-layouts: 6.26 us -> 3.95 us
    ppermute x12 -> x0, waiting for transfers between devices: 64.9 us -> none  [the longest x10 53 us: partner(): lax.ppermute(block, 'rows', [(i, i ^ 1 << step) for i in range(count)])]
    pallas_call x5 -> x1, Pallas kernels: 38 us -> 85.1 us  [sweep(): pl.pallas_call(functools.partial(sweep_kernel, row_count, col_count, bits...]
    ppermute x12 -> x0, starting transfers between devices: 16.4 us -> none  [the longest x10 11.6 us: partner(): lax.ppermute(block, 'rows', [(i, i ^ 1 << step) for i in range(count)])]
    pallas_call x1 -> x0, local copies, waits for them, and re-layouts: 1.51 us -> none  [finish(): pl.pallas_call(functools.partial(finish_kernel, count), out_shape=jax.Sha...]
    unnamed x7 -> x8, local copies, waits for them, and re-layouts: 4.31 us -> 3.95 us
  transfers between devices with their start and end apart: 12 -> 0, of which waited for: 10 -> 0; matrix products, arithmetic and copies ran while one was open for 0% -> 0% of each run, Pallas kernels for 6% -> 0%
where the time goes in v2:
time: 102 us
  Pallas kernels  97.8 us (96%)
  local copies, waits for them, and re-layouts  3.95 us (4%)
    pallas_call x1, Pallas kernels, sweep(): pl.pallas_call(functools.partial(sweep_kernel, row_count, col_count, bits...  85.1 us
    pallas_call x1, Pallas kernels, project(): pl.pallas_call(functools.partial(project_kernel, scales), out_shape=(jax....  9.36 us
    unnamed x8, local copies, waits for them, and re-layouts  3.95 us
    pallas_call x1, Pallas kernels, finish(): pl.pallas_call(functools.partial(finish_kernel, count), out_shape=jax.Sha...  3.3 us

profile of v2, /device:TPU:0, one launch (start us, length us, event | category | flops | bytes accessed | tf_op | source)
XLA Modules:
  0.0 101.8 jit_solution(15119887087296302753)
XLA Ops:
  0.0 0.0 copy-start
  0.0 1.7 %copy-done = f32[1024,576]{0,1:T(8,128)S(1)} copy-done((f32[1024,576]{0,1:T(8,128)S(1)}, f32[1024,576]{0,1:T(8,128)}, u32[]{:S(2)}) %copy-start) | copy-done | bytes 2359320
  1.7 0.0 copy-start.2
  1.7 1.6 %copy-done.2 = f32[4,1024,128]{2,1,0:T(8,128)S(1)} copy-done((f32[4,1024,128]{2,1,0:T(8,128)S(1)}, f32[4,1024,128]{2,1,0:T(8,128)}, u32[]{:S(2)}) %copy-start.2) | copy-done | bytes 2097176
  3.3 0.0 copy-start.3
  3.3 0.7 copy-done.3
  3.9 9.4 %shard_map.37 = (f32[512,384]{1,0:T(8,128)S(1)}, f32[512,256]{1,0:T(8,128)S(1)}) custom-call(f32[576,1024]{1,0:T(8,128)S(1)} %bitcast.3, f32[4,1024,128]{2,1,0:T(8,128)S(1)} %copy-done.2, s32[1,1024]{1,0:T(1,128)S(1)} %copy-done.3), custom_call_target="tpu_custom_call" | custom-call | tf_op jit(solution)/shard_map/pallas_call | solution.py:151
  13.3 0.0 copy-start.1
  13.3 85.1 %shard_map.38 = (f32[512,768]{1,0:T(8,128)S(1)}, f32[1,256,1024]{2,1,0:T(8,128)S(1)}) custom-call(f32[512,384]{1,0:T(8,128)S(1)} %get-tuple-element.9.refs_0_, f32[512,256]{1,0:T(8,128)S(1)} %get-tuple-element.10.refs_1_, f32[576,1024]{1,0:T(8,128)} %bitcast.2), custom_call_target="tpu_custom_call" | custom-call | tf_op jit(solution)/shard_map/pallas_call | solution.py:351
  98.4 0.0 copy-done.1
  98.5 3.3 %shard_map.39 = f32[320,1024]{1,0:T(8,128)} custom-call(f32[576,1024]{1,0:T(8,128)S(1)} %bitcast.4, f32[512,768]{1,0:T(8,128)S(1)} %get-tuple-element.11.coeff_ref, f32[1,256,1024]{2,1,0:T(8,128)S(1)} %get-tuple-element.12.blocks_ref), custom_call_target="tpu_custom_call" | custom-call | tf_op jit(solution)/shard_map/pallas_call | solution.py:409
Async XLA Ops:
  0.0 1.7 %copy-start = (f32[1024,576]{0,1:T(8,128)S(1)}, f32[1024,576]{0,1:T(8,128)}, u32[]{:S(2)}) copy-start(f32[1024,576]{0,1:T(8,128)} %param.3) | copy-start | bytes 7077892
  1.7 1.6 %copy-start.2 = (f32[4,1024,128]{2,1,0:T(8,128)S(1)}, f32[4,1024,128]{2,1,0:T(8,128)}, u32[]{:S(2)}) copy-start(f32[4,1024,128]{2,1,0:T(8,128)} %bases_ref.1) | copy-start | bytes 6291460
  3.3 0.7 copy-start.3
  13.3 85.1 %copy-start.1 = (f32[1024,576]{0,1:T(8,128)S(1)}, f32[1024,576]{0,1:T(8,128)}, u32[]{:S(2)}) copy-start(f32[1024,576]{0,1:T(8,128)} %param.3) | copy-start | bytes 7077892

commit v3 on v2

--- a/solution.py
+++ b/solution.py
@@ -169,13 +169,12 @@
 
 def sweep_kernel(row_count, col_count, bits, *refs):
     tgt_ref, own_ref, cols_ref, out_ref, blocks_ref = refs[:5]
-    work, peers, mine, theirs, held, landed, own_all, sib_all = refs[5:13]
-    peer_sems, block_sems, couple_sems, rest_sems, join_sems = refs[13:]
+    state, other, early, peers = refs[5:9]
+    peer_sems, block_sems, early_sems, link_sems, join_sems = refs[9:]
     row, col = lax.axis_index("rows"), lax.axis_index("cols")
-    width, half, wide = R // col_count, R // 2, LEVELS * R + TGT_PAD
+    width, basis_end = R // col_count, LEVELS * R
+    wide = basis_end + TGT_PAD
     core = lax.rem(row, 2)
-    my_half = pl.ds(pl.multiple_of(core * half, half), half)
-    other_half = pl.ds(pl.multiple_of((1 - core) * half, half), half)
     row_peers = []
     for step in range(row_count.bit_length() - 1):
         bit = lax.rem(row // (1 << step), 2)
@@ -228,124 +227,130 @@
                 source = lax.rem(col - apart + col_count, col_count)
                 part = spread_level(block, which, width, source)
                 total = part if total is None else total + part
-            work[at, which * R : (which + 1) * R] = total
-
-    work[:, LEVELS * R :] = tgt_ref[...]
+            state[0, at, which * R : (which + 1) * R] = total
+
+    def exchange(level, which, rows, cols):
+        first, count = rows
+        if bits[level] > 0 and which > 0:
+            count = count // 2
+            first = pl.multiple_of(first + core * count, R // 2)
+        region = (level, pl.ds(first, count), pl.ds(*cols))
+        copy = send(
+            state.at[region],
+            other.at[region],
+            link_sems.at[level, which],
+            row_peers[bits[level]],
+        )
+        return copy, region
+
+    def join(level, which, sent):
+        copy, region = sent
+        copy.wait()
+        if bits[level] == 0:
+            return None
+        part = other.at[region]
+        return send(part, part, join_sems.at[level, which], row_peers[0])
+
+    def joined(copy):
+        if copy is not None:
+            copy.wait()
+
+    def solve(level, apply, lo, hi):
+        at, mid = level_rows(level), slice(level * R, (level + 1) * R)
+        own_couple, sib_couple = state[level, at, mid], other[level, at, mid]
+        own_proj, sib_proj = state[level, at, lo:hi], other[level, at, lo:hi]
+        own = mul(apply, sib_proj - mul(sib_couple, own_proj))
+        out_ref[at, lo - (level + 1) * R : hi - (level + 1) * R] = own
+        if level == LEVELS - 1:
+            return
+        own, sib = halves(own), halves(own_proj - mul(own_couple, own))
+        for later in range(level + 1, LEVELS):
+            below = level_rows(later)
+            change = mul_halves(halves(state[level, below, mid]), own) + mul_halves(
+                halves(other[level, below, mid]), sib
+            )
+            state[level + 1, below, lo:hi] = (
+                state[level, below, lo:hi] + other[level, below, lo:hi] - change
+            )
+
+    state[0, :, basis_end:] = tgt_ref[...]
     gather(0)
+    if bits[0] > 0:
+        for level in range(1, LEVELS):
+            gather(level)
+        for step in range(bits[0]):
+            copy = send(state.at[0], early.at[step], early_sems.at[step], row_peers[step])
+            copy.wait()
+            state[0] += early[step]
+
     block_copies = []
+    couple = exchange(0, 0, (0, R), (0, R))
+    apply = tgt_join = None
     for level in range(LEVELS):
-        last = bits[level]
-        at, rest = level_rows(level), wide - (level + 1) * R
-        rest_cols = pl.ds((level + 1) * R, rest)
-
-        def couple_send(step):
-            return send(
-                mine.at[level, step],
-                theirs.at[level, step],
-                couple_sems.at[level, step],
-                row_peers[step],
-            )
-
-        mine[level, 0] = work[at, level * R : (level + 1) * R]
-        copy = couple_send(0)
+        start, following, left = level * R, (level + 1) * R, (LEVELS - 1 - level) * R
+        at, mid = level_rows(level), slice(start, following)
+        right_sent = lower_sent = None
+
+        def send_lower(level=level, following=following, left=left, start=start):
+            return exchange(level, 2, (following, left), (start, left + R))
+
+        if left > 0:
+            right_sent = exchange(level, 1, (start, R), (following, left))
+            if level > 0 or bits[0] > 0:
+                lower_sent = send_lower()
         if level > 0:
-            before = pl.ds((level - 1) * R, R)
-            below = pl.ds(level * R, (LEVELS - level) * R)
-            work[below, rest_cols] -= mul(work[below, before], coeffs_rest)
-        rest_copies = {}
-
-        def rest_send(step, src):
-            rest_copies[step] = send(
-                src,
-                landed.at[level, step, pl.ds(0, src.shape[0]), pl.ds(0, rest)],
-                rest_sems.at[level, step],
-                row_peers[step],
-            )
-
-        if last == 0:
-            rest_send(0, work.at[at, rest_cols])
-        else:
-            rest_send(0, work.at[pl.ds(pl.multiple_of(level * R + (1 - core) * half, half), half), rest_cols])
-        for step in range(last):
-            copy.wait()
-            mine[level, step + 1] = mine[level, step] + theirs[level, step]
-            copy = couple_send(step + 1)
-        copy.wait()
-        own_couple, sib_couple = mine[level, last], theirs[level, last]
-
-        def held_at(step):
-            return held.at[level, step, :, pl.ds(0, rest)]
-
-        def advance(step):
-            rest_copies[step].wait()
-            arrived = landed[level, step, pl.ds(0, half), pl.ds(0, rest)]
-            if step == 0:
-                rows = pl.ds(pl.multiple_of(level * R + core * half, half), half)
-                held[level, 0, :, pl.ds(0, rest)] = work[rows, rest_cols] + arrived
-            else:
-                held[level, step, :, pl.ds(0, rest)] = (
-                    held[level, step - 1, :, pl.ds(0, rest)] + arrived
-                )
-            rest_send(step + 1, held_at(step))
-
-        joins = []
-
-        def join():
-            rest_copies[last].wait()
-            ours = held_at(last - 1)
-            arrived = landed.at[level, last, pl.ds(0, half), pl.ds(0, rest)]
-            for k, (src, whole) in enumerate(((ours, own_all), (arrived, sib_all))):
-                place = whole.at[level, my_half, pl.ds(0, rest)]
-                joins.append(send(src, place, join_sems.at[level, k], row_peers[0]))
-                whole[level, my_half, pl.ds(0, rest)] = src[...]
-
-        between = [functools.partial(advance, step) for step in range(1, last)]
-        if last > 0:
-            advance(0)
-            between.append(join)
+            joined(tgt_join)
+            solve(level - 1, apply, basis_end, wide)
+        tgt_sent = exchange(level, 3, (start, left + R), (basis_end, TGT_PAD))
+        couple[0].wait()
+        own_couple, sib_couple = state[level, at, mid], other[level, at, mid]
         unit_row = lax.broadcasted_iota(jnp.int32, (R, R), 0)
         unit_col = lax.broadcasted_iota(jnp.int32, (R, R), 1)
         reduced = jnp.where(unit_row == unit_col, 1.0, 0.0) - mul_full(sib_couple, own_couple)
+        sent, joins = [lower_sent], []
+
+        def gather_rest():
+            for later in range(1, LEVELS):
+                gather(later)
+            sent[0] = send_lower()
+            src = cols_ref.at[pl.ds(TGT_DEV, cols_ref.shape[0] - TGT_DEV)]
+            for k, device in enumerate(col_peers):
+                block_copies.append(send(src, blocks_ref.at[k], block_sems.at[k], device))
+
+        def join_basis(level=level, right_sent=right_sent):
+            joins.append(join(level, 1, right_sent))
+            joins.append(join(level, 2, sent[0]))
+
+        between = []
+        if level == 0 and bits[0] == 0:
+            between = [gather_rest, lambda: None, lambda: None]
+        elif left > 0:
+            between = [lambda: None, lambda: None, join_basis]
         inverse = invert_spd(mul_full(reduced, reduced, COLS_ON_COLS), between)
         apply = mul_full(inverse, reduced, (((1,), (1,)), ((), ())))
-        if level == 0:
-            for later in range(1, LEVELS):
-                gather(later)
-            for k, device in enumerate(col_peers):
-                src = cols_ref.at[pl.ds(TGT_DEV, cols_ref.shape[0] - TGT_DEV)]
-                block_copies.append(send(src, blocks_ref.at[k], block_sems.at[k], device))
-        if last == 0:
-            rest_copies[0].wait()
-            own_proj = work[at, rest_cols]
-            sib_proj = landed[level, 0, :, pl.ds(0, rest)]
-        else:
-            for copy in joins:
-                copy.wait()
-            own_proj = own_all[level, :, pl.ds(0, rest)]
-            sib_proj = sib_all[level, :, pl.ds(0, rest)]
-
-        def coeffs_of(lo, hi):
-            right = sib_proj[:, lo:hi] - mul(sib_couple, own_proj[:, lo:hi])
-            return mul_full(apply, right)
-
-        if level < LEVELS - 1:
-            first = coeffs_of(0, R)
-            out_ref[at, :R] = first
-            below = pl.ds((level + 1) * R, (LEVELS - level - 1) * R)
-            work[below, (level + 1) * R : (level + 2) * R] -= mul(
-                work[below, level * R : (level + 1) * R], first
-            )
-            coeffs_rest = coeffs_of(R, rest)
-            out_ref[at, R:rest] = coeffs_rest
-        else:
-            out_ref[at, :rest] = coeffs_of(0, rest)
+        if level == 0 and bits[0] == 0:
+            join_basis()
+        for copy in joins:
+            joined(copy)
+        if left > 0:
+            solve(level, apply, following, following + R)
+            couple = exchange(level + 1, 0, (following, R), (following, R))
+        tgt_join = join(level, 3, tgt_sent)
+        if left > R:
+            solve(level, apply, following + R, basis_end)
+    joined(tgt_join)
+    solve(LEVELS - 1, apply, basis_end, wide)
+    if bits[0] > 0:
+        src = cols_ref.at[pl.ds(TGT_DEV, cols_ref.shape[0] - TGT_DEV)]
+        for k, device in enumerate(col_peers):
+            block_copies.append(send(src, blocks_ref.at[k], block_sems.at[k], device))
     for copy in block_copies:
         copy.wait()
 
 
 def sweep(row_count, col_count, bits, tgt, own_basis, columns):
-    wide, steps = LEVELS * R + TGT_PAD, row_count.bit_length() - 1
-    others = max(col_count - 1, 1)
+    wide = LEVELS * R + TGT_PAD
+    others, early = max(col_count - 1, 1), max(bits[0], 1)
     vmem = pl.BlockSpec(memory_space=pltpu.VMEM)
     hbm = pl.BlockSpec(memory_space=pl.ANY)
     return pl.pallas_call(
@@ -357,19 +362,15 @@
         in_specs=[vmem, vmem, hbm],
         out_specs=(vmem, hbm),
         scratch_shapes=[
-            pltpu.VMEM((LEVELS * R, wide), F32),
+            pltpu.VMEM((LEVELS, LEVELS * R, wide), F32),
+            pltpu.VMEM((LEVELS, LEVELS * R, wide), F32),
+            pltpu.VMEM((early, LEVELS * R if bits[0] else 8, wide), F32),
             pltpu.VMEM((others,) + own_basis.shape, F32),
-            pltpu.VMEM((LEVELS, steps, R, R), F32),
-            pltpu.VMEM((LEVELS, steps, R, R), F32),
-            pltpu.VMEM((LEVELS, steps, R // 2, wide - R), F32),
-            pltpu.VMEM((LEVELS, steps, R, wide - R), F32),
-            pltpu.VMEM((LEVELS, R, wide - R), F32),
-            pltpu.VMEM((LEVELS, R, wide - R), F32),
             pltpu.SemaphoreType.DMA((others, LEVELS, 2)),
             pltpu.SemaphoreType.DMA((others, 2)),
-            pltpu.SemaphoreType.DMA((LEVELS, steps, 2)),
-            pltpu.SemaphoreType.DMA((LEVELS, steps, 2)),
-            pltpu.SemaphoreType.DMA((LEVELS, 2, 2)),
+            pltpu.SemaphoreType.DMA((early, 2)),
+            pltpu.SemaphoreType.DMA((LEVELS, 4, 2)),
+            pltpu.SemaphoreType.DMA((LEVELS, 4, 2)),
         ],
         compiler_params=pltpu.CompilerParams(
             collective_id=0, has_side_effects=True, vmem_limit_bytes=VMEM_BYTES

time: 102 us -> 86.2 us (0.85)
  Pallas kernels: 97.8 us -> 82 us
    pallas_call x1, Pallas kernels: 85.1 us -> 69.4 us  [sweep(): pl.pallas_call(functools.partial(sweep_kernel, row_count, col_count, bits...]
where the time goes in v3:
time: 86.2 us; the launch traced here: 86 us
  Pallas kernels  82 us (95%)
  local copies, waits for them, and re-layouts  3.95 us (5%)
    pallas_call x1, Pallas kernels, sweep(): pl.pallas_call(functools.partial(sweep_kernel, row_count, col_count, bits...  69.4 us
    pallas_call x1, Pallas kernels, project(): pl.pallas_call(functools.partial(project_kernel, scales), out_shape=(jax....  9.36 us
    unnamed x8, local copies, waits for them, and re-layouts  3.95 us
    pallas_call x1, Pallas kernels, finish(): pl.pallas_call(functools.partial(finish_kernel, count), out_shape=jax.Sha...  3.3 us

profile of v3, /device:TPU:0, one launch (start us, length us, event | category | flops | bytes accessed | tf_op | source)
XLA Modules:
  0.0 86.0 jit_solution(52136137718780276)
XLA Ops:
  0.0 0.0 copy-start
  0.0 1.7 %copy-done = f32[1024,576]{0,1:T(8,128)S(1)} copy-done((f32[1024,576]{0,1:T(8,128)S(1)}, f32[1024,576]{0,1:T(8,128)}, u32[]{:S(2)}) %copy-start) | copy-done | bytes 2359320
  1.7 0.0 copy-start.2
  1.7 1.6 %copy-done.2 = f32[4,1024,128]{2,1,0:T(8,128)S(1)} copy-done((f32[4,1024,128]{2,1,0:T(8,128)S(1)}, f32[4,1024,128]{2,1,0:T(8,128)}, u32[]{:S(2)}) %copy-start.2) | copy-done | bytes 2097176
  3.3 0.0 copy-start.3
  3.3 0.7 copy-done.3
  3.9 9.4 %shard_map.37 = (f32[512,384]{1,0:T(8,128)S(1)}, f32[512,256]{1,0:T(8,128)S(1)}) custom-call(f32[576,1024]{1,0:T(8,128)S(1)} %bitcast.3, f32[4,1024,128]{2,1,0:T(8,128)S(1)} %copy-done.2, s32[1,1024]{1,0:T(1,128)S(1)} %copy-done.3), custom_call_target="tpu_custom_call" | custom-call | tf_op jit(solution)/shard_map/pallas_call | solution.py:151
  13.3 0.0 copy-start.1
  13.3 69.4 %shard_map.38 = (f32[512,768]{1,0:T(8,128)S(1)}, f32[1,256,1024]{2,1,0:T(8,128)S(1)}) custom-call(f32[512,384]{1,0:T(8,128)S(1)} %get-tuple-element.9.refs_0_, f32[512,256]{1,0:T(8,128)S(1)} %get-tuple-element.10.refs_1_, f32[576,1024]{1,0:T(8,128)} %bitcast.2), custom_call_target="tpu_custom_call" | custom-call | tf_op jit(solution)/shard_map/pallas_call | solution.py:356
  82.7 0.0 copy-done.1
  82.7 3.3 %shard_map.39 = f32[320,1024]{1,0:T(8,128)} custom-call(f32[576,1024]{1,0:T(8,128)S(1)} %bitcast.4, f32[512,768]{1,0:T(8,128)S(1)} %get-tuple-element.11.coeff_ref, f32[1,256,1024]{2,1,0:T(8,128)S(1)} %get-tuple-element.12.blocks_ref), custom_call_target="tpu_custom_call" | custom-call | tf_op jit(solution)/shard_map/pallas_call | solution.py:410
Async XLA Ops:
  0.0 1.7 %copy-start = (f32[1024,576]{0,1:T(8,128)S(1)}, f32[1024,576]{0,1:T(8,128)}, u32[]{:S(2)}) copy-start(f32[1024,576]{0,1:T(8,128)} %param.3) | copy-start | bytes 7077892
  1.7 1.6 %copy-start.2 = (f32[4,1024,128]{2,1,0:T(8,128)S(1)}, f32[4,1024,128]{2,1,0:T(8,128)}, u32[]{:S(2)}) copy-start(f32[4,1024,128]{2,1,0:T(8,128)} %bases_ref.1) | copy-start | bytes 6291460
  3.3 0.7 copy-start.3
  13.3 69.4 %copy-start.1 = (f32[1024,576]{0,1:T(8,128)S(1)}, f32[1024,576]{0,1:T(8,128)}, u32[]{:S(2)}) copy-start(f32[1024,576]{0,1:T(8,128)} %param.3) | copy-start | bytes 7077892

commit v4 on v3

--- a/solution.py
+++ b/solution.py
@@ -44,11 +44,11 @@
 
 
 def invert_two(a, b, d):
-    ia = 1.0 / a
-    t = b * ia
-    low = 1.0 / (d - b * t)
-    mid = -t * low
-    return ia - t * mid, mid, low
+    det = a * d - b * b
+    over = pl.reciprocal(det, approx=True)
+    over = over * (2.0 - det * over)
+    over = over * (2.0 - det * over)
+    return d * over, -b * over, a * over
 
 
 def invert_four(d):
@@ -73,24 +73,23 @@
     ]
 
 
-def sweep_four(tiles, first):
+def sweep_four(tiles, which, sub_first):
     lane = lax.broadcasted_iota(jnp.int32, (8, LANES), 1)
     sub = lax.broadcasted_iota(jnp.int32, (8, LANES), 0)
+    first = 8 * which + sub_first
     spread = [
         [jnp.broadcast_to(tile[:, first + j : first + j + 1], (8, LANES)) for j in range(4)]
         for tile in tiles
     ]
-    pivot = [
-        [jnp.broadcast_to(spread[0][j][first + i : first + i + 1], (8, LANES)) for j in range(4)]
-        for i in range(4)
-    ]
+
+    def row_of(value, i):
+        return jnp.broadcast_to(value[sub_first + i : sub_first + i + 1], (8, LANES))
+
+    pivot = [[row_of(spread[which][j], i) for j in range(4)] for i in range(4)]
     inverse = invert_four(pivot)
+    inside = (lane >= first) & (lane < first + 4)
     rows = [
-        jnp.where(
-            (lane >= first) & (lane < first + 4),
-            jnp.where(lane == first + j, 1.0, 0.0),
-            jnp.broadcast_to(tiles[0][first + j : first + j + 1], (8, LANES)),
-        )
+        jnp.where(inside, jnp.where(lane == first + j, 1.0, 0.0), row_of(tiles[which], j))
         for j in range(4)
     ]
     solved = [
@@ -98,62 +97,84 @@
         + (inverse[i][2] * rows[2] + inverse[i][3] * rows[3])
         for i in range(4)
     ]
-    kept = (lane < first) | (lane >= first + 4)
     out = []
     for tile, cols in zip(tiles, spread):
         change = (cols[0] * solved[0] + cols[1] * solved[1]) + (
             cols[2] * solved[2] + cols[3] * solved[3]
         )
-        out.append(jnp.where(kept, tile, 0.0) - change)
+        out.append(jnp.where(inside, 0.0, tile) - change)
     for i in range(4):
-        out[0] = jnp.where(sub == first + i, solved[i], out[0])
+        out[which] = jnp.where(sub == sub_first + i, solved[i], out[which])
     return out
 
 
-def invert_spd(gram, between):
-    count = R // 8
+def invert_spd(gram, cut, between):
+    group = 2
+    count = R // (8 * group)
 
     def body(_, tiles):
-        tiles = sweep_four(list(tiles), 0)
-        tiles = sweep_four(tiles, 4)
-        tiles = tiles[1:] + tiles[:1]
-        return tuple(pltpu.roll(tile, LANES - 8, 1) for tile in tiles)
-
-    tiles = tuple(gram[8 * i : 8 * i + 8] for i in range(count))
-    parts = len(between) + 1
-    for part in range(parts):
-        tiles = lax.fori_loop(count * part // parts, count * (part + 1) // parts, body, tiles)
-        if part < len(between):
-            between[part]()
+        tiles = list(tiles)
+        for which in range(group):
+            tiles = sweep_four(tiles, which, 0)
+            tiles = sweep_four(tiles, which, 4)
+        tiles = tiles[group:] + tiles[:group]
+        return tuple(pltpu.roll(tile, LANES - 8 * group, 1) for tile in tiles)
+
+    tiles = tuple(gram[8 * i : 8 * i + 8] for i in range(R // 8))
+    if cut > 0:
+        tiles = lax.fori_loop(0, cut, body, tiles)
+        between()
+    tiles = lax.fori_loop(cut, count, body, tiles)
     return jnp.concatenate(tiles, axis=0)
 
 
-def project_kernel(scales, cols_ref, bases_ref, order_ref, tgt_ref, own_ref):
+def project_kernel(scales, cols_hbm, bases_hbm, order_ref, tgt_ref, own_ref, cols_ref, bases_ref, sems):
     rows = cols_ref.shape[1]
+    copies = [pltpu.make_async_copy(bases_hbm.at[0:2], bases_ref.at[0:2], sems.at[0])]
+    copies.append(pltpu.make_async_copy(cols_hbm, cols_ref, sems.at[1]))
+    copies.append(pltpu.make_async_copy(bases_hbm.at[2:4], bases_ref.at[2:4], sems.at[2]))
+    for copy in copies:
+        copy.start()
     place = lax.broadcasted_iota(jnp.int32, (rows, rows), 0)
     pick = jnp.where(place == order_ref[...], 1.0, 0.0).astype(BF16)
-    cols = halves(cols_ref[...])
-    for level in range(LEVELS):
-        high, low = halves(bases_ref[level])
+    copies[0].wait()
+    cols = None
+    for pair in range(0, LEVELS, 2):
+        if pair > 0:
+            copies[2].wait()
+        both = jnp.concatenate([bases_ref[pair], bases_ref[pair + 1]], axis=1)
+        high, low = halves(both)
         high = jnp.dot(pick, high, preferred_element_type=F32).astype(BF16)
         low = jnp.dot(pick, low, preferred_element_type=F32).astype(BF16)
-        at = pl.ds(level * R, R)
-        found = scales[level] * mul_halves(cols, (high, low))
-        tgt_ref[at, :] = found[:TGT_PAD].T
-        basis = found[TGT_DEV:]
-        if basis.shape[0] < LANES:
-            short = LANES - basis.shape[0]
-            basis = jnp.concatenate([basis, jnp.zeros((short, R), F32)], axis=0)
-        own_ref[at, :] = basis.T
+        if cols is None:
+            copies[1].wait()
+            cols = halves(cols_ref[...])
+        products = mul_halves(cols, (high, low))
+        for level in range(pair, pair + 2):
+            at = pl.ds(level * R, R)
+            found = scales[level] * products[:, (level - pair) * R : (level - pair + 1) * R]
+            tgt_ref[at, :] = found[:TGT_PAD].T
+            basis = found[TGT_DEV:]
+            if basis.shape[0] < LANES:
+                short = LANES - basis.shape[0]
+                basis = jnp.concatenate([basis, jnp.zeros((short, R), F32)], axis=0)
+            own_ref[at, :] = basis.T
 
 
 def project(scales, columns, row_bases, order):
+    hbm = pl.BlockSpec(memory_space=pltpu.HBM)
     return pl.pallas_call(
         functools.partial(project_kernel, scales),
         out_shape=(
             jax.ShapeDtypeStruct((LEVELS * R, TGT_PAD), F32),
             jax.ShapeDtypeStruct((LEVELS * R, max(columns.shape[0] - TGT_DEV, LANES)), F32),
         ),
+        in_specs=[hbm, hbm, pl.BlockSpec(memory_space=pltpu.VMEM)],
+        scratch_shapes=[
+            pltpu.VMEM(columns.shape, F32),
+            pltpu.VMEM(row_bases.shape, F32),
+            pltpu.SemaphoreType.DMA((3,)),
+        ],
         compiler_params=pltpu.CompilerParams(vmem_limit_bytes=VMEM_BYTES),
     )(columns, row_bases, order)
 
@@ -255,23 +276,29 @@
         if copy is not None:
             copy.wait()
 
-    def solve(level, apply, lo, hi):
-        at, mid = level_rows(level), slice(level * R, (level + 1) * R)
-        own_couple, sib_couple = state[level, at, mid], other[level, at, mid]
-        own_proj, sib_proj = state[level, at, lo:hi], other[level, at, lo:hi]
-        own = mul(apply, sib_proj - mul(sib_couple, own_proj))
-        out_ref[at, lo - (level + 1) * R : hi - (level + 1) * R] = own
-        if level == LEVELS - 1:
-            return
-        own, sib = halves(own), halves(own_proj - mul(own_couple, own))
-        for later in range(level + 1, LEVELS):
-            below = level_rows(later)
-            change = mul_halves(halves(state[level, below, mid]), own) + mul_halves(
-                halves(other[level, below, mid]), sib
+    def stacked(level):
+        below = pl.ds((level + 1) * R, (LEVELS - 1 - level) * R)
+        mid = slice(level * R, (level + 1) * R)
+        return halves(
+            jnp.concatenate([state[level, below, mid], other[level, below, mid]], axis=1)
+        )
+
+    def update(level, left_side, own, sib, lo, hi):
+        out_ref[level_rows(level), lo - (level + 1) * R : hi - (level + 1) * R] = own
+        if level < LEVELS - 1:
+            below = pl.ds((level + 1) * R, (LEVELS - 1 - level) * R)
+            both = halves(jnp.concatenate([own, sib], axis=0))
+            state[level + 1, below, lo:hi] = (
+                state[level, below, lo:hi]
+                + other[level, below, lo:hi]
+                - mul_halves(left_side, both)
             )
-            state[level + 1, below, lo:hi] = (
-                state[level, below, lo:hi] + other[level, below, lo:hi] - change
-            )
+
+    def solve(level, whole, left_side, lo, hi):
+        at = level_rows(level)
+        right = jnp.concatenate([other[level, at, lo:hi], state[level, at, lo:hi]], axis=0)
+        both = mul_halves(whole, halves(right))
+        update(level, left_side, both[:R], both[R:], lo, hi)
 
     state[0, :, basis_end:] = tgt_ref[...]
     gather(0)
@@ -285,7 +312,7 @@
 
     block_copies = []
     couple = exchange(0, 0, (0, R), (0, R))
-    apply = tgt_join = None
+    whole = left_side = tgt_join = None
     for level in range(LEVELS):
         start, following, left = level * R, (level + 1) * R, (LEVELS - 1 - level) * R
         at, mid = level_rows(level), slice(start, following)
@@ -300,7 +327,7 @@
                 lower_sent = send_lower()
         if level > 0:
             joined(tgt_join)
-            solve(level - 1, apply, basis_end, wide)
+            solve(level - 1, whole, left_side, basis_end, wide)
         tgt_sent = exchange(level, 3, (start, left + R), (basis_end, TGT_PAD))
         couple[0].wait()
         own_couple, sib_couple = state[level, at, mid], other[level, at, mid]
@@ -321,25 +348,44 @@
             joins.append(join(level, 1, right_sent))
             joins.append(join(level, 2, sent[0]))
 
-        between = []
+        cut, between = 0, None
         if level == 0 and bits[0] == 0:
-            between = [gather_rest, lambda: None, lambda: None]
+            cut, between = 2, gather_rest
         elif left > 0:
-            between = [lambda: None, lambda: None, join_basis]
-        inverse = invert_spd(mul_full(reduced, reduced, COLS_ON_COLS), between)
-        apply = mul_full(inverse, reduced, (((1,), (1,)), ((), ())))
+            cut, between = 6, join_basis
+        top = jnp.max(jnp.abs(reduced), axis=0, keepdims=True)
+        shrink = 1.0 / jnp.maximum(jnp.max(top, axis=1, keepdims=True), 1e-30)
+        reduced = reduced * shrink
+        inverse = invert_spd(mul_full(reduced, reduced, COLS_ON_COLS), cut, between)
+        apply = shrink * mul_full(inverse, reduced, (((1,), (1,)), ((), ())))
         if level == 0 and bits[0] == 0:
             join_basis()
         for copy in joins:
             joined(copy)
         if left > 0:
-            solve(level, apply, following, following + R)
+            left_side = stacked(level)
+            cols = pl.ds(following, R)
+            own_proj = state[level, at, cols]
+            own = mul(apply, other[level, at, cols] - mul(sib_couple, own_proj))
+            sib = own_proj - mul(own_couple, own)
+            update(level, left_side, own, sib, following, following + R)
             couple = exchange(level + 1, 0, (following, R), (following, R))
         tgt_join = join(level, 3, tgt_sent)
+        turned = mul(apply, sib_couple)
+        upper = jnp.concatenate([apply, -turned], axis=1)
+        lower = -mul(own_couple, upper)
+        lower = jnp.concatenate(
+            [lower[:, :R], jnp.where(unit_row == unit_col, 1.0, 0.0) + lower[:, R:]], axis=1
+        )
+        whole = halves(jnp.concatenate([upper, lower], axis=0))
         if left > R:
-            solve(level, apply, following + R, basis_end)
+            solve(level, whole, left_side, following + R, basis_end)
     joined(tgt_join)
-    solve(LEVELS - 1, apply, basis_end, wide)
+    at = level_rows(LEVELS - 1)
+    right = jnp.concatenate(
+        [other[LEVELS - 1, at, basis_end:], state[LEVELS - 1, at, basis_end:]], axis=0
+    )
+    out_ref[at, :TGT_PAD] = mul(upper, right)
     if bits[0] > 0:
         src = cols_ref.at[pl.ds(TGT_DEV, cols_ref.shape[0] - TGT_DEV)]
         for k, device in enumerate(col_peers):

time: 86.2 us -> 83.3 us (0.966)
  Pallas kernels: 82 us -> 79.1 us
    pallas_call x1, Pallas kernels: 69.4 us -> 67.4 us  [sweep(): pl.pallas_call(functools.partial(sweep_kernel, row_count, col_count, bits...]
    pallas_call x1, Pallas kernels: 9.36 us -> 8.45 us  [project(): pl.pallas_call(functools.partial(project_kernel, scales), out_shape=(jax....]
where the time goes in v4:
time: 83.3 us; the launch traced here: 83.1 us
  Pallas kernels  79.1 us (95%)
  local copies, waits for them, and re-layouts  3.95 us (5%)
    pallas_call x1, Pallas kernels, sweep(): pl.pallas_call(functools.partial(sweep_kernel, row_count, col_count, bits...  67.4 us
    pallas_call x1, Pallas kernels, project(): pl.pallas_call(functools.partial(project_kernel, scales), out_shape=(jax....  8.45 us
    unnamed x8, local copies, waits for them, and re-layouts  3.95 us
    pallas_call x1, Pallas kernels, finish(): pl.pallas_call(functools.partial(finish_kernel, count), out_shape=jax.Sha...  3.3 us

profile of v4, /device:TPU:0, one launch (start us, length us, event | category | flops | bytes accessed | tf_op | source)
XLA Modules:
  0.0 83.1 jit_solution(15401879350475282122)
XLA Ops:
  0.0 0.0 copy-start
  0.0 1.7 %copy-done = f32[1024,576]{0,1:T(8,128)S(1)} copy-done((f32[1024,576]{0,1:T(8,128)S(1)}, f32[1024,576]{0,1:T(8,128)}, u32[]{:S(2)}) %copy-start) | copy-done | bytes 2359320
  1.7 0.0 copy-start.2
  1.7 1.6 %copy-done.2 = f32[4,1024,128]{2,1,0:T(8,128)S(1)} copy-done((f32[4,1024,128]{2,1,0:T(8,128)S(1)}, f32[4,1024,128]{2,1,0:T(8,128)}, u32[]{:S(2)}) %copy-start.2) | copy-done | bytes 2097176
  3.3 0.0 copy-start.3
  3.3 0.7 copy-done.3
  3.9 8.4 %shard_map.37 = (f32[512,384]{1,0:T(8,128)S(1)}, f32[512,256]{1,0:T(8,128)S(1)}) custom-call(f32[576,1024]{1,0:T(8,128)S(1)} %bitcast.3, f32[4,1024,128]{2,1,0:T(8,128)S(1)} %copy-done.2, s32[1,1024]{1,0:T(1,128)S(1)} %copy-done.3), custom_call_target="tpu_custom_call" | custom-call | tf_op jit(solution)/shard_map/pallas_call | solution.py:166
  12.4 0.0 copy-start.1
  12.4 67.4 %shard_map.38 = (f32[512,768]{1,0:T(8,128)S(1)}, f32[1,256,1024]{2,1,0:T(8,128)S(1)}) custom-call(f32[512,384]{1,0:T(8,128)S(1)} %get-tuple-element.9.refs_0_, f32[512,256]{1,0:T(8,128)S(1)} %get-tuple-element.10.refs_1_, f32[576,1024]{1,0:T(8,128)} %bitcast.2), custom_call_target="tpu_custom_call" | custom-call | tf_op jit(solution)/shard_map/pallas_call | solution.py:402
  79.8 0.0 copy-done.1
  79.8 3.3 %shard_map.39 = f32[320,1024]{1,0:T(8,128)} custom-call(f32[576,1024]{1,0:T(8,128)S(1)} %bitcast.4, f32[512,768]{1,0:T(8,128)S(1)} %get-tuple-element.11.coeff_ref, f32[1,256,1024]{2,1,0:T(8,128)S(1)} %get-tuple-element.12.blocks_ref), custom_call_target="tpu_custom_call" | custom-call | tf_op jit(solution)/shard_map/pallas_call | solution.py:456
Async XLA Ops:
  0.0 1.7 %copy-start = (f32[1024,576]{0,1:T(8,128)S(1)}, f32[1024,576]{0,1:T(8,128)}, u32[]{:S(2)}) copy-start(f32[1024,576]{0,1:T(8,128)} %param.3) | copy-start | bytes 7077892
  1.7 1.6 %copy-start.2 = (f32[4,1024,128]{2,1,0:T(8,128)S(1)}, f32[4,1024,128]{2,1,0:T(8,128)}, u32[]{:S(2)}) copy-start(f32[4,1024,128]{2,1,0:T(8,128)} %bases_hbm.1) | copy-start | bytes 6291460
  3.3 0.7 copy-start.3
  12.4 67.4 %copy-start.1 = (f32[1024,576]{0,1:T(8,128)S(1)}, f32[1024,576]{0,1:T(8,128)}, u32[]{:S(2)}) copy-start(f32[1024,576]{0,1:T(8,128)} %param.3) | copy-start | bytes 7077892

commit v5 on v4

--- a/solution.py
+++ b/solution.py
@@ -14,6 +14,7 @@
 LANES = 128
 TGT_PAD = -(-TGT_DEV // LANES) * LANES
 VMEM_BYTES = 48 * 1024 * 1024
+PROJECT_BYTES = 62 * 1024 * 1024
 F32 = jnp.float32
 BF16 = jnp.bfloat16
 
@@ -108,7 +109,7 @@
     return out
 
 
-def invert_spd(gram, cut, between):
+def invert_spd(gram, between):
     group = 2
     count = R // (8 * group)
 
@@ -121,10 +122,12 @@
         return tuple(pltpu.roll(tile, LANES - 8 * group, 1) for tile in tiles)
 
     tiles = tuple(gram[8 * i : 8 * i + 8] for i in range(R // 8))
-    if cut > 0:
-        tiles = lax.fori_loop(0, cut, body, tiles)
-        between()
-    tiles = lax.fori_loop(cut, count, body, tiles)
+    done = 0
+    for cut, action in between:
+        tiles = lax.fori_loop(done, cut, body, tiles)
+        action()
+        done = cut
+    tiles = lax.fori_loop(done, count, body, tiles)
     return jnp.concatenate(tiles, axis=0)
 
 
@@ -175,7 +178,7 @@
             pltpu.VMEM(row_bases.shape, F32),
             pltpu.SemaphoreType.DMA((3,)),
         ],
-        compiler_params=pltpu.CompilerParams(vmem_limit_bytes=VMEM_BYTES),
+        compiler_params=pltpu.CompilerParams(vmem_limit_bytes=PROJECT_BYTES),
     )(columns, row_bases, order)
 
 
@@ -189,9 +192,9 @@
 
 
 def sweep_kernel(row_count, col_count, bits, *refs):
-    tgt_ref, own_ref, cols_ref, out_ref, blocks_ref = refs[:5]
-    state, other, early, peers = refs[5:9]
-    peer_sems, block_sems, early_sems, link_sems, join_sems = refs[9:]
+    tgt_hbm, own_hbm, cols_ref, out_ref, blocks_ref = refs[:5]
+    state, other, early, peers, own_ref = refs[5:10]
+    load_sems, peer_sems, block_sems, early_sems, link_sems, join_sems = refs[10:]
     row, col = lax.axis_index("rows"), lax.axis_index("cols")
     width, basis_end = R // col_count, LEVELS * R
     wide = basis_end + TGT_PAD
@@ -214,12 +217,19 @@
         copy.start()
         return copy
 
+    own_load = pltpu.make_async_copy(own_hbm, own_ref, load_sems.at[0])
+    own_load.start()
+    tgt_load = pltpu.make_async_copy(
+        tgt_hbm, state.at[0, :, pl.ds(basis_end, TGT_PAD)], load_sems.at[1]
+    )
+    tgt_load.start()
     barrier = pltpu.get_barrier_semaphore()
     for device in row_peers + col_peers:
         pl.semaphore_signal(
             barrier, inc=1, device_id=device, device_id_type=pl.DeviceIdType.MESH
         )
     pl.semaphore_wait(barrier, len(row_peers) + len(col_peers))
+    own_load.wait()
 
     def level_rows(level):
         return pl.ds(level * R, R)
@@ -300,8 +310,8 @@
         both = mul_halves(whole, halves(right))
         update(level, left_side, both[:R], both[R:], lo, hi)
 
-    state[0, :, basis_end:] = tgt_ref[...]
     gather(0)
+    tgt_load.wait()
     if bits[0] > 0:
         for level in range(1, LEVELS):
             gather(level)
@@ -325,10 +335,20 @@
             right_sent = exchange(level, 1, (start, R), (following, left))
             if level > 0 or bits[0] > 0:
                 lower_sent = send_lower()
-        if level > 0:
-            joined(tgt_join)
-            solve(level - 1, whole, left_side, basis_end, wide)
-        tgt_sent = exchange(level, 3, (start, left + R), (basis_end, TGT_PAD))
+        late, tgt = level == 2, {}
+
+        def targets(level=level, whole=whole, left_side=left_side, start=start, left=left, tgt=tgt):
+            if level > 0:
+                joined(tgt_join)
+                solve(level - 1, whole, left_side, basis_end, wide)
+            tgt["sent"] = exchange(level, 3, (start, left + R), (basis_end, TGT_PAD))
+
+        if not late:
+            targets()
+        if level == 2:
+            src = cols_ref.at[pl.ds(TGT_DEV, cols_ref.shape[0] - TGT_DEV)]
+            for k, device in enumerate(col_peers):
+                block_copies.append(send(src, blocks_ref.at[k], block_sems.at[k], device))
         couple[0].wait()
         own_couple, sib_couple = state[level, at, mid], other[level, at, mid]
         unit_row = lax.broadcasted_iota(jnp.int32, (R, R), 0)
@@ -340,23 +360,27 @@
             for later in range(1, LEVELS):
                 gather(later)
             sent[0] = send_lower()
-            src = cols_ref.at[pl.ds(TGT_DEV, cols_ref.shape[0] - TGT_DEV)]
-            for k, device in enumerate(col_peers):
-                block_copies.append(send(src, blocks_ref.at[k], block_sems.at[k], device))
 
         def join_basis(level=level, right_sent=right_sent):
             joins.append(join(level, 1, right_sent))
             joins.append(join(level, 2, sent[0]))
 
-        cut, between = 0, None
+        between = []
         if level == 0 and bits[0] == 0:
-            cut, between = 2, gather_rest
+            between.append((2, gather_rest))
         elif left > 0:
-            cut, between = 6, join_basis
+            between.append((6, join_basis))
+        if late:
+
+            def join_targets(level=level, sent_before=tgt_sent):
+                nonlocal tgt_join
+                tgt_join = join(level - 1, 3, sent_before)
+
+            between = [(2, join_targets), (4, targets)] + between
         top = jnp.max(jnp.abs(reduced), axis=0, keepdims=True)
         shrink = 1.0 / jnp.maximum(jnp.max(top, axis=1, keepdims=True), 1e-30)
         reduced = reduced * shrink
-        inverse = invert_spd(mul_full(reduced, reduced, COLS_ON_COLS), cut, between)
+        inverse = invert_spd(mul_full(reduced, reduced, COLS_ON_COLS), between)
         apply = shrink * mul_full(inverse, reduced, (((1,), (1,)), ((), ())))
         if level == 0 and bits[0] == 0:
             join_basis()
@@ -370,7 +394,9 @@
             sib = own_proj - mul(own_couple, own)
             update(level, left_side, own, sib, following, following + R)
             couple = exchange(level + 1, 0, (following, R), (following, R))
-        tgt_join = join(level, 3, tgt_sent)
+        tgt_sent = tgt["sent"]
+        if level != 1:
+            tgt_join = join(level, 3, tgt_sent)
         turned = mul(apply, sib_couple)
         upper = jnp.concatenate([apply, -turned], axis=1)
         lower = -mul(own_couple, upper)
@@ -386,10 +412,6 @@
         [other[LEVELS - 1, at, basis_end:], state[LEVELS - 1, at, basis_end:]], axis=0
     )
     out_ref[at, :TGT_PAD] = mul(upper, right)
-    if bits[0] > 0:
-        src = cols_ref.at[pl.ds(TGT_DEV, cols_ref.shape[0] - TGT_DEV)]
-        for k, device in enumerate(col_peers):
-            block_copies.append(send(src, blocks_ref.at[k], block_sems.at[k], device))
     for copy in block_copies:
         copy.wait()
 
@@ -405,13 +427,15 @@
             jax.ShapeDtypeStruct((LEVELS * R, wide - R), F32),
             jax.ShapeDtypeStruct((others, columns.shape[0] - TGT_DEV, columns.shape[1]), F32),
         ),
-        in_specs=[vmem, vmem, hbm],
+        in_specs=[pl.BlockSpec(memory_space=pltpu.HBM)] * 2 + [hbm],
         out_specs=(vmem, hbm),
         scratch_shapes=[
             pltpu.VMEM((LEVELS, LEVELS * R, wide), F32),
             pltpu.VMEM((LEVELS, LEVELS * R, wide), F32),
             pltpu.VMEM((early, LEVELS * R if bits[0] else 8, wide), F32),
             pltpu.VMEM((others,) + own_basis.shape, F32),
+            pltpu.VMEM(own_basis.shape, F32),
+            pltpu.SemaphoreType.DMA((2,)),
             pltpu.SemaphoreType.DMA((others, LEVELS, 2)),
             pltpu.SemaphoreType.DMA((others, 2)),
             pltpu.SemaphoreType.DMA((early, 2)),

time: 83.3 us -> 84.3 us (1.012)
  Pallas kernels: 79.1 us -> 81.7 us
  local copies, waits for them, and re-layouts: 3.95 us -> 2.33 us
    pallas_call x1, Pallas kernels: 8.45 us -> 10.5 us  [project(): pl.pallas_call(functools.partial(project_kernel, scales), out_shape=(jax....]
    unnamed x8 -> x6, local copies, waits for them, and re-layouts: 3.95 us -> 2.33 us
where the time goes in v5:
time: 84.3 us; the launch traced here: 84.1 us
  Pallas kernels  81.7 us (97%)
  local copies, waits for them, and re-layouts  2.33 us (3%)
    pallas_call x1, Pallas kernels, sweep(): pl.pallas_call(functools.partial(sweep_kernel, row_count, col_count, bits...  67.9 us
    pallas_call x1, Pallas kernels, project(): pl.pallas_call(functools.partial(project_kernel, scales), out_shape=(jax....  10.5 us
    pallas_call x1, Pallas kernels, finish(): pl.pallas_call(functools.partial(finish_kernel, count), out_shape=jax.Sha...  3.3 us
    unnamed x6, local copies, waits for them, and re-layouts  2.33 us

profile of v5, /device:TPU:0, one launch (start us, length us, event | category | flops | bytes accessed | tf_op | source)
XLA Modules:
  0.0 84.1 jit_solution(11227129296490528739)
XLA Ops:
  0.0 10.5 %shard_map.37 = (f32[512,384]{1,0:T(8,128)}, f32[512,256]{1,0:T(8,128)}) custom-call(f32[576,1024]{1,0:T(8,128)} %bitcast.2, f32[4,1024,128]{2,1,0:T(8,128)} %bases_hbm.1, s32[1,1024]{1,0:T(1,128)} %order_ref.1), custom_call_target="tpu_custom_call" | custom-call | tf_op jit(solution)/shard_map/pallas_call | solution.py:169
  10.5 0.0 copy-start
  10.5 0.0 copy-start.1
  10.5 1.3 %copy-done.1 = f32[512,384]{1,0:T(8,128)S(1)} copy-done((f32[512,384]{1,0:T(8,128)S(1)}, f32[512,384]{1,0:T(8,128)}, u32[]{:S(2)}) %copy-start.1) | copy-done | bytes 786456
  11.8 0.0 copy-start.2
  11.8 1.0 %copy-done.2 = f32[512,256]{1,0:T(8,128)S(1)} copy-done((f32[512,256]{1,0:T(8,128)S(1)}, f32[512,256]{1,0:T(8,128)}, u32[]{:S(2)}) %copy-start.2) | copy-done | bytes 524312
  12.9 67.9 %shard_map.38 = (f32[512,768]{1,0:T(8,128)S(1)}, f32[1,256,1024]{2,1,0:T(8,128)S(1)}) custom-call(f32[512,384]{1,0:T(8,128)S(1)} %copy-done.1, f32[512,256]{1,0:T(8,128)S(1)} %copy-done.2, f32[576,1024]{1,0:T(8,128)} %bitcast.3), custom_call_target="tpu_custom_call" | custom-call | tf_op jit(solution)/shard_map/pallas_call | solution.py:424
  80.8 0.0 copy-done
  80.8 3.3 %shard_map.39 = f32[320,1024]{1,0:T(8,128)} custom-call(f32[576,1024]{1,0:T(8,128)S(1)} %bitcast.4, f32[512,768]{1,0:T(8,128)S(1)} %get-tuple-element.11.coeff_ref, f32[1,256,1024]{2,1,0:T(8,128)S(1)} %get-tuple-element.12.blocks_ref), custom_call_target="tpu_custom_call" | custom-call | tf_op jit(solution)/shard_map/pallas_call | solution.py:480
Async XLA Ops:
  10.5 70.3 %copy-start = (f32[1024,576]{0,1:T(8,128)S(1)}, f32[1024,576]{0,1:T(8,128)}, u32[]{:S(2)}) copy-start(f32[1024,576]{0,1:T(8,128)} %param.3) | copy-start | bytes 7077892
  10.5 1.3 %copy-start.1 = (f32[512,384]{1,0:T(8,128)S(1)}, f32[512,384]{1,0:T(8,128)}, u32[]{:S(2)}) copy-start(f32[512,384]{1,0:T(8,128)} %get-tuple-element.9.refs_0_) | copy-start | bytes 2359300
  11.8 1.0 %copy-start.2 = (f32[512,256]{1,0:T(8,128)S(1)}, f32[512,256]{1,0:T(8,128)}, u32[]{:S(2)}) copy-start(f32[512,256]{1,0:T(8,128)} %get-tuple-element.10.refs_1_) | copy-start | bytes 1572868

commit v6 on v5

--- a/solution.py
+++ b/solution.py
@@ -14,7 +14,6 @@
 LANES = 128
 TGT_PAD = -(-TGT_DEV // LANES) * LANES
 VMEM_BYTES = 48 * 1024 * 1024
-PROJECT_BYTES = 62 * 1024 * 1024
 F32 = jnp.float32
 BF16 = jnp.bfloat16
 
@@ -114,11 +113,18 @@
     count = R // (8 * group)
 
     def body(_, tiles):
-        tiles = list(tiles)
+        panel, others = list(tiles[:group]), tiles[group:]
         for which in range(group):
-            tiles = sweep_four(tiles, which, 0)
-            tiles = sweep_four(tiles, which, 4)
-        tiles = tiles[group:] + tiles[:group]
+            panel = sweep_four(panel, which, 0)
+            panel = sweep_four(panel, which, 4)
+        lane = lax.broadcasted_iota(jnp.int32, (8, LANES), 1)
+        left_side = jnp.concatenate(others, axis=0)[:, : 8 * group]
+        change = mul_full(left_side, jnp.concatenate(panel, axis=0))
+        others = [
+            jnp.where(lane < 8 * group, 0.0, tile) - change[8 * i : 8 * i + 8]
+            for i, tile in enumerate(others)
+        ]
+        tiles = others + panel
         return tuple(pltpu.roll(tile, LANES - 8 * group, 1) for tile in tiles)
 
     tiles = tuple(gram[8 * i : 8 * i + 8] for i in range(R // 8))
@@ -178,7 +184,7 @@
             pltpu.VMEM(row_bases.shape, F32),
             pltpu.SemaphoreType.DMA((3,)),
         ],
-        compiler_params=pltpu.CompilerParams(vmem_limit_bytes=PROJECT_BYTES),
+        compiler_params=pltpu.CompilerParams(vmem_limit_bytes=VMEM_BYTES),
     )(columns, row_bases, order)
 
 

time: 84.3 us -> 82.1 us (0.974)
  Pallas kernels: 81.7 us -> 78 us
  local copies, waits for them, and re-layouts: 2.33 us -> 3.95 us
    pallas_call x1, Pallas kernels: 10.5 us -> 8.45 us  [project(): pl.pallas_call(functools.partial(project_kernel, scales), out_shape=(jax....]
    pallas_call x1, Pallas kernels: 67.9 us -> 66.2 us  [sweep(): pl.pallas_call(functools.partial(sweep_kernel, row_count, col_count, bits...]
    unnamed x6 -> x8, local copies, waits for them, and re-layouts: 2.33 us -> 3.95 us
where the time goes in v6:
time: 82.1 us; the launch traced here: 81.9 us
  Pallas kernels  78 us (95%)
  local copies, waits for them, and re-layouts  3.95 us (5%)
    pallas_call x1, Pallas kernels, sweep(): pl.pallas_call(functools.partial(sweep_kernel, row_count, col_count, bits...  66.2 us
    pallas_call x1, Pallas kernels, project(): pl.pallas_call(functools.partial(project_kernel, scales), out_shape=(jax....  8.45 us
    unnamed x8, local copies, waits for them, and re-layouts  3.95 us
    pallas_call x1, Pallas kernels, finish(): pl.pallas_call(functools.partial(finish_kernel, count), out_shape=jax.Sha...  3.3 us

profile of v6, /device:TPU:0, one launch (start us, length us, event | category | flops | bytes accessed | tf_op | source)
XLA Modules:
  0.0 81.9 jit_solution(7791930579866641838)
XLA Ops:
  0.0 0.0 copy-start
  0.0 1.7 %copy-done = f32[1024,576]{0,1:T(8,128)S(1)} copy-done((f32[1024,576]{0,1:T(8,128)S(1)}, f32[1024,576]{0,1:T(8,128)}, u32[]{:S(2)}) %copy-start) | copy-done | bytes 2359320
  1.7 0.0 copy-start.2
  1.7 1.6 %copy-done.2 = f32[4,1024,128]{2,1,0:T(8,128)S(1)} copy-done((f32[4,1024,128]{2,1,0:T(8,128)S(1)}, f32[4,1024,128]{2,1,0:T(8,128)}, u32[]{:S(2)}) %copy-start.2) | copy-done | bytes 2097176
  3.3 0.0 copy-start.3
  3.3 0.7 copy-done.3
  3.9 8.4 %shard_map.37 = (f32[512,384]{1,0:T(8,128)S(1)}, f32[512,256]{1,0:T(8,128)S(1)}) custom-call(f32[576,1024]{1,0:T(8,128)S(1)} %bitcast.3, f32[4,1024,128]{2,1,0:T(8,128)S(1)} %copy-done.2, s32[1,1024]{1,0:T(1,128)S(1)} %copy-done.3), custom_call_target="tpu_custom_call" | custom-call | tf_op jit(solution)/shard_map/pallas_call | solution.py:175
  12.4 0.0 copy-start.1
  12.4 66.2 %shard_map.38 = (f32[512,768]{1,0:T(8,128)S(1)}, f32[1,256,1024]{2,1,0:T(8,128)S(1)}) custom-call(f32[512,384]{1,0:T(8,128)S(1)} %get-tuple-element.9.refs_0_, f32[512,256]{1,0:T(8,128)S(1)} %get-tuple-element.10.refs_1_, f32[576,1024]{1,0:T(8,128)} %bitcast.2), custom_call_target="tpu_custom_call" | custom-call | tf_op jit(solution)/shard_map/pallas_call | solution.py:430
  78.6 0.0 copy-done.1
  78.6 3.3 %shard_map.39 = f32[320,1024]{1,0:T(8,128)} custom-call(f32[576,1024]{1,0:T(8,128)S(1)} %bitcast.4, f32[512,768]{1,0:T(8,128)S(1)} %get-tuple-element.11.coeff_ref, f32[1,256,1024]{2,1,0:T(8,128)S(1)} %get-tuple-element.12.blocks_ref), custom_call_target="tpu_custom_call" | custom-call | tf_op jit(solution)/shard_map/pallas_call | solution.py:486
Async XLA Ops:
  0.0 1.7 %copy-start = (f32[1024,576]{0,1:T(8,128)S(1)}, f32[1024,576]{0,1:T(8,128)}, u32[]{:S(2)}) copy-start(f32[1024,576]{0,1:T(8,128)} %param.3) | copy-start | bytes 7077892
  1.7 1.6 %copy-start.2 = (f32[4,1024,128]{2,1,0:T(8,128)S(1)}, f32[4,1024,128]{2,1,0:T(8,128)}, u32[]{:S(2)}) copy-start(f32[4,1024,128]{2,1,0:T(8,128)} %bases_hbm.1) | copy-start | bytes 6291460
  3.3 0.7 copy-start.3
  12.4 66.2 %copy-start.1 = (f32[1024,576]{0,1:T(8,128)S(1)}, f32[1024,576]{0,1:T(8,128)}, u32[]{:S(2)}) copy-start(f32[1024,576]{0,1:T(8,128)} %param.3) | copy-start | bytes 7077892
